TPU v7x, 256 devices: a whole 4x4x8 slice. The times are simulated.
256 devices in a mesh: gx: 8 (over x, core), gy: 32 (over z, y).
Axes of the slice: x: 4, y: 4, z: 8, core: 2. Of those that a mesh axis runs over, the one named last changes fastest.
Arguments:
- charges: bfloat16 [524288, 32], P(('gx', 'gy')), may hold values from -6 to 6
- panel_counts: int32 [8192], P(('gx', 'gy')), may hold values from 1 to 64, as said below
- basis: bfloat16 [8192, 64, 64], P(('gx', 'gy')), may hold values from -0.75 to 0.75
- transfer: bfloat16 [8192, 64, 64], P(('gx', 'gy')), may hold values from -0.5 to 0.5
- leaf_coupling: bfloat16 [8192, 16, 64, 64], P(('gx', 'gy')), may hold values from -0.1875 to 0.1875
- leaf_partners: int32 [8192, 16], P(('gx', 'gy')), may hold values from 0 to 8191, as said below
- near_blocks: bfloat16 [8192, 3, 64, 64], P(('gx', 'gy')), may hold values from -0.4375 to 0.4375
- parent_coupling: bfloat16 [4096, 16, 64, 64], P(('gx', 'gy')), may hold values from -0.1875 to 0.1875
- parent_partners: int32 [4096, 16], P(('gx', 'gy')), may hold values from 0 to 4095, as said below
Outputs:
- potential: bfloat16 [524288, 32], P(('gx', 'gy'))
Inputs may be any that keep to these rules, and one draw needn't show every extreme that they name: `panel_counts`: every value 1 to 64 occurs; every fifth leaf has all 64 panels live. `leaf_partners`: the partner of leaf g lies among the leaves of g's device, the device before or the device after in the order of the combined index gx * 32 + gy (leaf g is on device g // 32). `parent_partners`: the partner of parent q lies in the same block of 512 parents as q (one index of gx).
All inputs are finite; a program needn't handle non-finite values.
Results may differ from a plain program's by a relative error of at most 0.0054.
Values may be sent and summed in bfloat16 or wider, within the bound.
A program may use at most 128 MiB of HBM per device.

v0:
```python
import jax
import jax.numpy as jnp
from jax import lax
from jax.sharding import PartitionSpec as P


def shifted(array, axis, by):
    length = lax.axis_size(axis)
    pairs = [(i, i + by) for i in range(length) if 0 <= i + by < length]
    return lax.ppermute(array, axis, pairs)


def send_rims(payload, offset):
    return shifted(payload, ("gx", "gy"), offset)


def per_device(
    charges,
    panel_counts,
    basis,
    transfer,
    leaf_coupling,
    leaf_partners,
    near_blocks,
    parent_coupling,
    parent_partners,
):
    leaves, leaf_size, rank = basis.shape
    sides = charges.shape[1]
    half = leaves // 2
    slots = jnp.arange(leaf_size, dtype=jnp.int32)
    mask = (slots[None, :] < panel_counts[:, None]).astype(jnp.bfloat16)[:, :, None]
    live = charges.reshape(leaves, leaf_size, sides) * mask
    leaf_coef = jnp.einsum("gpk,gpr->gkr", basis, live, preferred_element_type=jnp.float32).astype(
        jnp.bfloat16
    )
    pairs = transfer.reshape(half, 2, rank, rank)
    kids = leaf_coef.reshape(half, 2, rank, sides)
    parent_coef = jnp.einsum(
        "qckl,qckr->qlr", pairs, kids, preferred_element_type=jnp.float32
    ).astype(jnp.bfloat16)
    device = lax.axis_index("gx") * lax.axis_size("gy") + lax.axis_index("gy")
    relative = leaf_partners - device * leaves
    cut = leaves * rank
    flat_coef = leaf_coef.reshape(cut, sides)
    received = []
    for offset in (1, -1):
        edge = live[leaves - 1] if offset == 1 else live[0]
        payload = jnp.concatenate([flat_coef, edge], axis=0)
        received.append(send_rims(payload, offset))
    before, after = received
    window_coef = jnp.concatenate([before[:cut], flat_coef, after[:cut]], axis=0).reshape(
        3 * leaves, rank, sides
    )
    picked = window_coef[relative + leaves]
    leaf_far = jnp.einsum(
        "gjkl,gjlr->gkr", leaf_coupling, picked, preferred_element_type=jnp.float32
    )
    row_start = lax.axis_index("gx") * lax.axis_size("gy") * half
    row_coef = lax.all_gather(parent_coef, "gy", axis=0, tiled=True)
    chosen = row_coef[parent_partners - row_start]
    parent_far = jnp.einsum(
        "qjkl,qjlr->qkr", parent_coupling, chosen, preferred_element_type=jnp.float32
    )
    parent_far = parent_far.astype(jnp.bfloat16)
    spread = jnp.repeat(parent_far, 2, axis=0)
    local_coef = (
        leaf_far + jnp.einsum("gkl,glr->gkr", transfer, spread, preferred_element_type=jnp.float32)
    ).astype(jnp.bfloat16)
    window = jnp.concatenate([before[cut:][None], live, after[cut:][None]], axis=0)
    near = jnp.zeros((leaves, leaf_size, sides), jnp.float32)
    for n in range(3):
        near = near + jnp.einsum(
            "gpq,gqr->gpr",
            near_blocks[:, n],
            window[n : n + leaves],
            preferred_element_type=jnp.float32,
        )
    total = jnp.einsum("gpk,gkr->gpr", basis, local_coef, preferred_element_type=jnp.float32) + near
    total = total * mask.astype(jnp.float32)
    return total.astype(jnp.bfloat16).reshape(leaves * leaf_size, sides)


def solution(mesh):
    in_specs = (
        P(("gx", "gy"), None),
        P(("gx", "gy")),
        P(("gx", "gy"), None, None),
        P(("gx", "gy"), None, None),
        P(("gx", "gy"), None, None, None),
        P(("gx", "gy"), None),
        P(("gx", "gy"), None, None, None),
        P(("gx", "gy"), None, None, None),
        P(("gx", "gy"), None),
    )
    out_specs = P(("gx", "gy"), None)
    return jax.shard_map(
        per_device, mesh=mesh, in_specs=in_specs, out_specs=out_specs, check_vma=False
    )
```

profile of v0, /device:TPU:8, one launch (start us, length us, event | category | flops | bytes accessed | tf_op | source)
XLA Modules:
  0.0 116.7 jit_solution(10312674021182058005)
XLA Ops:
  6.5 0.0 copy-start
  6.5 0.0 copy-start.2
  6.5 0.0 copy-start.3
  6.5 0.0 all-gather.2.cloned.1.call-start
  6.5 0.8 fusion.23
  7.3 1.2 %reshape.62 = bf16[32,64,32]{1,0,2:T(8,128)(2,1)S(1)} reshape(bf16[2048,32]{0,1:T(8,128)(2,1)} %param.9) | data formatting | bytes 262144 | tf_op jit(solution)/shard_map/reshape | solution.py:33
  8.5 0.1 copy_multiply_fusion
  8.6 1.3 %convolution_convert_fusion = bf16[32,32,64]{2,1,0:T(8,128)(2,1)S(1)} fusion(bf16[32,64,32]{1,2,0:T(8,128)(2,1)S(1)} %copy_multiply_fusion, bf16[32,64,64]{2,1,0:T(8,128)(2,1)} %param.11), kind=kOutput, calls=%fused_computation.10 | convolution fusion | flops 8454144 | bytes 524288 | tf_op jit(solution)/shard_map/gpk,gpr->gkr/dot_general | solution.py:34
  9.9 0.0 copy-done
  9.9 1.0 fusion.7
  10.9 0.0 all-gather.2.cloned.1.call-update
  10.9 0.1 copy.24
  11.0 0.3 reshape.63
  11.3 4.1 %collective-permute-start.1 = (bf16[2112,32]{0,1:T(8,128)(2,1)S(1)}, bf16[2112,32]{0,1:T(8,128)(2,1)S(1)}, u32[]{:S(2)}, u32[]{:S(2)}) collective-permute-start(bf16[2112,32]{0,1:T(8,128)(2,1)S(1)} %get-tuple-element.7), channel_id=1, source_target_pairs={{1,0},{2,1},{3,2},{4,3},{5,4},{6,5},{7,6},{8,7},{9,8},{10,9},{11,1... | collective-permute-start | bytes 405512 | tf_op jit(solution)/shard_map/ppermute | solution.py:10
  15.4 1.9 %collective-permute-start = (bf16[2112,32]{0,1:T(8,128)(2,1)S(1)}, bf16[2112,32]{0,1:T(8,128)(2,1)S(1)}, u32[]{:S(2)}, u32[]{:S(2)}) collective-permute-start(bf16[2112,32]{0,1:T(8,128)(2,1)S(1)} %get-tuple-element.8), channel_id=1, source_target_pairs={{0,1},{1,2},{2,3},{3,4},{4,5},{5,6},{6,7},{7,8},{8,9},{9,10},{10,1... | collective-permute-start | bytes 405512 | tf_op jit(solution)/shard_map/ppermute | solution.py:10
  17.4 0.0 copy-done.2
  17.4 0.1 reshape.79
  17.5 0.0 copy-done.3
  17.5 1.4 %fusion.10 = f32[32,32,64]{2,1,0:T(8,128)S(1)} fusion(bf16[32,64,32]{1,2,0:T(8,128)(2,1)S(1)} %copy_multiply_fusion, bf16[32,3,64,64]{3,2,1,0:T(8,128)(2,1)} %param.15), kind=kOutput, calls=%fused_computation.19 | convolution fusion | flops 8388608 | bytes 917504 | tf_op jit(solution)/shard_map/gpq,gqr->gpr/dot_general | solution.py:73
  18.9 0.1 copy.25
  19.0 0.1 reshape.71
  19.1 0.0 collective-permute-done.1
  19.1 3.3 %collective-permute-done = bf16[2112,32]{0,1:T(8,128)(2,1)S(1)} collective-permute-done((bf16[2112,32]{0,1:T(8,128)(2,1)S(1)}, bf16[2112,32]{0,1:T(8,128)(2,1)S(1)}, u32[]{:S(2)}, u32[]{:S(2)}) %collective-permute-start) | collective-permute-done | bytes 135200 | tf_op jit(solution)/shard_map/ppermute | solution.py:10
  22.4 0.8 reshape.64
  23.2 0.3 copy.26
  23.5 3.5 %gather_fusion = bf16[512,64,32]{1,2,0:T(8,128)(2,1)} fusion(bf16[96,64,32]{1,2,0:T(8,128)(2,1)S(1)} %copy.26, s32[1024]{0:T(1024)S(1)} %pad_clamp_fusion.1), kind=kCustom, calls=%fused_computation | custom fusion | bytes 4196352 | tf_op jit(solution)/shard_map/gather | solution.py:55
  27.1 1.4 %convolution_add_fusion.2 = f32[32,32,64]{2,1,0:T(8,128)S(1)} fusion(f32[32,32,64]{2,1,0:T(8,128)S(1)} %fusion.10, bf16[32,3,64,64]{3,2,1,0:T(8,128)(2,1)} %param.15, bf16[32,64,32]{1,2,0:T(8,128)(2,1)S(1)} %copy_multiply_fusion, bf16[1,64,32]{1,2,0:T(8,128)(2,1)S(1)} %slice_bitcast_fusion.1), kind=kOutput, calls=%fused_computation.7 | convolution fusion | flops 8724480 | bytes 1183744 | tf_op jit(solution)/shard_map/gpq,gqr->gpr/dot_general | solution.py:73
  28.5 2.3 %convolution_add_fusion.1 = f32[32,32,64]{2,1,0:T(8,128)} fusion(f32[32,32,64]{2,1,0:T(8,128)S(1)} %convolution_add_fusion.2, bf16[32,3,64,64]{3,2,1,0:T(8,128)(2,1)} %param.15, bf16[1,64,32]{1,2,0:T(8,128)(2,1)S(1)} %slice_bitcast_fusion, bf16[32,64,32]{1,2,0:T(8,128)(2,1)S(1)} %copy_multiply_fusion), kind=kOutput, calls=%fused_computation.6 | convolution fusion | flops 8724480 | bytes 1183744 | tf_op jit(solution)/shard_map/gpq,gqr->gpr/dot_general | solution.py:73
  30.8 63.7 %all-gather.2.cloned.1.call-done = bf16[512,64,32]{1,2,0:T(8,128)(2,1)} async-done(((bf16[16,64,32]{1,2,0:T(8,128)(2,1)}), bf16[512,64,32]{1,2,0:T(8,128)(2,1)}) %all-gather.2.cloned.1.call-update) | async-done | bytes 2097168 | tf_op jit(solution)/shard_map/all_gather | solution.py:60
  94.5 3.2 %gather_fusion.1 = bf16[256,64,32]{1,2,0:T(8,128)(2,1)S(1)} fusion(bf16[512,64,32]{1,2,0:T(8,128)(2,1)} %all-gather.2.cloned.1.call-done, s32[1024]{0:T(1024)S(1)} %pad_clamp_fusion), kind=kCustom, calls=%fused_computation.1 | custom fusion | bytes 2098176 | tf_op jit(solution)/shard_map/gather | solution.py:61
  97.7 0.0 copy-start.1
  97.7 3.4 %fusion.8 = bf16[16,64,32]{1,2,0:T(8,128)(2,1)S(1)} fusion(bf16[16,16,64,32]{2,3,1,0:T(8,128)(2,1)S(1)} %bitcast.83, bf16[16,16,64,64]{3,2,1,0:T(8,128)(2,1)} %param.16), kind=kOutput, calls=%fused_computation.17 | convolution fusion | flops 67141632 | bytes 3211264 | tf_op jit(solution)/shard_map/qjkl,qjlr->qkr/dot_general | solution.py:62
  101.2 0.1 broadcast_in_dim.20
  101.2 0.4 fusion.26
  101.6 0.0 copy-done.1
  101.6 7.2 %fusion.4 = bf16[32,64,32]{1,2,0:T(8,128)(2,1)S(1)} fusion(f32[32,32,64]{2,1,0:T(8,128)} %convolution_add_fusion.1, bf16[32,64,64]{2,1,0:T(8,128)(2,1)S(1)} %copy-done.1, f32[32,32,64]{2,1,0:T(8,128)S(1)} %fusion.26, bf16[32,16,64,32]{2,3,1,0:T(8,128)(2,1)} %bitcast.82, bf16[32,16,64,64]{3,2,1,0:T(8,128)(2,1)} %param.13, f32[32,64]{1,0:T(8,128)S(1)} %get-tuple-element.9), kind=kOutput, calls=%fused_computation.11 | convolution fusion | flops 142934016 | bytes 7217152 | tf_op jit(solution)/shard_map/gpk,gkr->gpr/dot_general | solution.py:79
  108.8 0.1 copy.30
  108.9 0.9 reshape.68
  (11 shorter events, 0.1 us)
Async XLA Ops:
  6.5 3.4 %copy-start = (bf16[32,64,64]{2,1,0:T(8,128)(2,1)S(1)}, bf16[32,64,64]{2,1,0:T(8,128)(2,1)}, u32[]{:S(2)}) copy-start(bf16[32,64,64]{2,1,0:T(8,128)(2,1)} %param.12) | copy-start | bytes 786436
  6.5 10.8 %copy-start.2 = (s32[16,16]{1,0:T(8,128)S(1)}, s32[16,16]{1,0:T(8,128)}, u32[]{:S(2)}) copy-start(s32[16,16]{1,0:T(8,128)} %param.17) | copy-start | bytes 3076
  6.5 10.9 %copy-start.3 = (s32[32,16]{0,1:T(8,128)S(1)}, s32[32,16]{0,1:T(8,128)}, u32[]{:S(2)}) copy-start(s32[32,16]{0,1:T(8,128)} %param.14) | copy-start | bytes 6148
  6.5 88.0 %all-gather.2.cloned.1.call-start = ((), (), s32[]{:S(2)}) async-start(), calls=%async_computation | async-start | bytes 4325376 | tf_op jit(solution)/shard_map/all_gather | solution.py:60
  11.3 7.8 %collective-permute-start.1 = (bf16[2112,32]{0,1:T(8,128)(2,1)S(1)}, bf16[2112,32]{0,1:T(8,128)(2,1)S(1)}, u32[]{:S(2)}, u32[]{:S(2)}) collective-permute-start(bf16[2112,32]{0,1:T(8,128)(2,1)S(1)} %get-tuple-element.7), channel_id=1, source_target_pairs={{1,0},{2,1},{3,2},{4,3},{5,4},{6,5},{7,6},{8,7},{9,8},{10,9},{11,1... | collective-permute-start | bytes 405512 | tf_op jit(solution)/shard_map/ppermute | solution.py:10
  15.4 6.9 %collective-permute-start = (bf16[2112,32]{0,1:T(8,128)(2,1)S(1)}, bf16[2112,32]{0,1:T(8,128)(2,1)S(1)}, u32[]{:S(2)}, u32[]{:S(2)}) collective-permute-start(bf16[2112,32]{0,1:T(8,128)(2,1)S(1)} %get-tuple-element.8), channel_id=1, source_target_pairs={{0,1},{1,2},{2,3},{3,4},{4,5},{5,6},{6,7},{7,8},{8,9},{9,10},{10,1... | collective-permute-start | bytes 405512 | tf_op jit(solution)/shard_map/ppermute | solution.py:10
  97.7 3.9 %copy-start.1 = (bf16[32,64,64]{2,1,0:T(8,128)(2,1)S(1)}, bf16[32,64,64]{2,1,0:T(8,128)(2,1)}, u32[]{:S(2)}) copy-start(bf16[32,64,64]{2,1,0:T(8,128)(2,1)} %param.11) | copy-start | bytes 786436
Sparse Core Ops, SparseCore 0:
  11.0 83.4 all-gather.1
where the time goes:
time: 118 us; the launch traced here: 117 us
  waiting for transfers between devices  67 us (57%)
  matrix products  18.4 us (16%)
  between operations  13.6 us (12%)
  local copies, waits for them, and re-layouts  10.8 us (9%)
  starting transfers between devices  6.02 us (5%)
    all_gather x1, waiting for transfers between devices, per_device(): row_coef = lax.all_gather(parent_coef, 'gy', axis=0, tiled=True)  63.7 us
    dot_general x1, matrix products, per_device(): jnp.einsum('gpk,gkr->gpr', basis, local_coef, preferred_element_type=jnp....  7.2 us
    ppermute x2, starting transfers between devices, shifted(): return lax.ppermute(array, axis, pairs)  6.01 us
    dot_general x3, matrix products, per_device(): jnp.einsum('gpq,gqr->gpr', near_blocks[:, n], window[n:n + leaves], prefe...  5.12 us
    gather x1, local copies, waits for them, and re-layouts, per_device(): picked = window_coef[relative + leaves]  3.54 us
    dot_general x1, matrix products, per_device(): jnp.einsum('qjkl,qjlr->qkr', parent_coupling, chosen, preferred_element_t...  3.44 us
    ppermute x2, waiting for transfers between devices, shifted(): return lax.ppermute(array, axis, pairs)  3.26 us
    gather x1, local copies, waits for them, and re-layouts, per_device(): chosen = row_coef[parent_partners - row_start]  3.18 us
  transfers between devices with their start and end apart: 3, of which 2 were waited for; matrix products, arithmetic and copies ran while one was open for 9% of the time, Pallas kernels for 0%

commit v1 on v0

v1 whole, which is shorter than its diff:
```python
import jax
import jax.numpy as jnp
from jax import lax
from jax.experimental import pallas as pl
from jax.experimental.pallas import tpu as pltpu
from jax.sharding import PartitionSpec as P

BF = jnp.bfloat16
F32 = jnp.float32
MESH = pl.DeviceIdType.MESH

NY = 4
NZ = 8
NGX = 8
NGY = NY * NZ
LD = 32
QD = 16
TD = QD // 2
ROW_TILES = NGY * TD
R = 32
WIN = 4

SPAN = {"A": (0, 4), "A0": (0, 2), "A1": (2, 2), "B": (4, 4), "B0": (4, 2), "B1": (6, 2)}


def children(dy, dz, part):
    out = []
    if part == "A":
        if dz == 0:
            if dy == 0:
                out += [("y+", 1, 0, "A"), ("y-", -1, 0, "A")]
            if dy == 1:
                out += [("y+", 2, 0, "A0")]
            if dy == -1:
                out += [("y-", 2, 0, "A1")]
            out += [("z+", dy, 1, "A"), ("z-", dy, -1, "A")]
        elif dz in (1, 2):
            out += [("z+", dy, dz + 1, "A")]
        elif dz in (-1, -2):
            out += [("z-", dy, dz - 1, "A")]
        elif dz == 3:
            out += [("z+", dy, 4, "A0")]
        elif dz == -3:
            out += [("z-", dy, 4, "A1")]
    if part == "B":
        if dy == 0:
            if dz in (0, 1, 2):
                out += [("z+", 0, dz + 1, "B")]
            if dz in (0, -1, -2):
                out += [("z-", 0, dz - 1, "B")]
            if dz == 3:
                out += [("z+", 0, 4, "B0")]
            if dz == -3:
                out += [("z-", 0, 4, "B1")]
            out += [("y+", 1, dz, "B"), ("y-", -1, dz, "B")]
        elif dy == 1:
            out += [("y+", 2, dz, "B0")]
        elif dy == -1:
            out += [("y-", 2, dz, "B1")]
    return out


STEPS = (
    ((1, 0, "A"),), ((-1, 0, "A"),), ((0, 1, "B"),), ((0, -1, "B"),),
    ((1, 0, "B"),), ((-1, 0, "B"),), ((0, 1, "A"),), ((0, -1, "A"),),
    ((1, 1, "A"),), ((1, -1, "A"),), ((-1, 1, "A"),), ((-1, -1, "A"),),
    ((0, 2, "B"),), ((0, -2, "B"),), ((2, 0, "A0"), (2, 0, "A1")),
    ((0, 2, "A"),), ((0, -2, "A"),), ((1, 1, "B"),), ((-1, 1, "B"),),
    ((1, 2, "A"),), ((1, -2, "A"),), ((1, -1, "B"),), ((-1, -1, "B"),),
    ((-1, 2, "A"),), ((-1, -2, "A"),), ((2, 0, "B0"), (2, 0, "B1")),
    ((0, 3, "B"),), ((0, -3, "B"),), ((1, 2, "B"),), ((-1, 2, "B"),),
    ((2, 1, "A"),), ((2, -1, "A"),), ((1, -2, "B"),), ((-1, -2, "B"),),
    ((2, 1, "B0"), (2, 1, "B1")), ((0, 3, "A"),), ((0, -3, "A"),),
    ((2, -1, "B0"), (2, -1, "B1")), ((1, 3, "A"),), ((1, -3, "A"),),
    ((1, 3, "B"),), ((-1, 3, "B"),), ((-1, 3, "A"),), ((-1, -3, "A"),),
    ((1, -3, "B"),), ((-1, -3, "B"),), ((0, 4, "B0"), (0, 4, "B1")),
    ((2, 2, "B0"), (2, 2, "B1")), ((2, -2, "B0"), (2, -2, "B1")),
    ((2, 2, "A"),), ((2, -2, "A"),), ((2, 3, "B0"), (2, 3, "B1")),
    ((0, 4, "A0"), (0, 4, "A1")), ((1, 4, "A0"), (1, 4, "A1")),
    ((2, -3, "B0"), (2, -3, "B1")), ((-1, 4, "A0"), (-1, 4, "A1")),
    ((1, 4, "B"),), ((-1, 4, "B"),), ((2, 3, "A"),), ((2, -3, "A"),),
    ((2, 4, "B0"), (2, 4, "B1")), ((2, 4, "A0"), (2, 4, "A1")),
)
MESSAGES = tuple(m for step in STEPS for m in step)
NUMBER = {m: i for i, m in enumerate(MESSAGES)}


def dot_nn(a, b):
    return lax.dot_general(a, b, (((1,), (0,)), ((), ())), preferred_element_type=F32)


def dot_nt(a, b):
    return lax.dot_general(a, b, (((1,), (1,)), ((), ())), preferred_element_type=F32)


def kernel(
    ch_hbm, cnt_hbm, basis_hbm, transfer_hbm, lc_hbm, lp_hbm, nb_hbm, pc_hbm, pp_hbm,
    out_ref,
    ch, basis, transfer, lc, nb, pc, cnt, lp, pp,
    live, win, row, cpl, bdiag, near, far,
    in_sem, recv_sem, send_sem, rim_recv, rim_send,
):
    gx = lax.axis_index("gx")
    gy = lax.axis_index("gy")
    z = gy // NY
    y = gy % NY
    dev = gx * NGY + gy
    total = NGX * NGY
    prv = (dev + total - 1) % total
    nxt = (dev + 1) % total
    prv_id = (prv // NGY, prv % NGY)
    nxt_id = (nxt // NGY, nxt % NGY)
    ids = {
        "y+": (gx, z * NY + (y + 1) % NY),
        "y-": (gx, z * NY + (y + NY - 1) % NY),
        "z+": (gx, ((z + 1) % NZ) * NY + y),
        "z-": (gx, ((z + NZ - 1) % NZ) * NY + y),
    }

    loads = [
        pltpu.make_async_copy(s, d, in_sem.at[i])
        for i, (s, d) in enumerate(
            [
                (ch_hbm, ch), (cnt_hbm, cnt), (basis_hbm, basis), (transfer_hbm, transfer),
                (nb_hbm, nb), (lp_hbm, lp), (pp_hbm, pp), (lc_hbm, lc), (pc_hbm, pc),
            ]
        )
    ]
    for load in loads:
        load.start()

    barrier = pltpu.get_barrier_semaphore()
    for d in (ids["y+"], ids["y-"], ids["z+"], ids["z-"], prv_id, nxt_id):
        pl.semaphore_signal(barrier, inc=1, device_id=d, device_id_type=MESH)

    mine, before, after = ((d % WIN) * QD for d in (dev, prv, nxt))

    lane = lax.broadcasted_iota(jnp.int32, (R, 128), 1)
    low = lane < 64

    def masks(q):
        return lane < cnt[2 * q], (lane >= 64) & (lane < cnt[2 * q + 1] + 64)

    def swap(tile):
        return jnp.concatenate([tile[:, 64:], tile[:, :64]], axis=1)

    for load in loads[:4]:
        load.wait()

    zero = jnp.zeros((R, 128), BF)
    parents = []
    for q in range(QD):
        m0, m1 = masks(q)
        tile = ch[:, 128 * q : 128 * q + 128]
        l0 = jnp.where(m0, tile, zero)
        l1 = jnp.where(m1, tile, zero)
        live[q + 1] = l0 + l1
        coef = dot_nn(jnp.concatenate([l0, l1], axis=0), basis[2 * q : 2 * q + 2].reshape(128, 64))
        coef = coef.astype(BF)
        pair = jnp.concatenate([coef[:R], coef[R:]], axis=1)
        win[0, mine + q] = pair
        win[1, mine + q] = jnp.concatenate([coef[R:], coef[:R]], axis=1)
        parents.append(dot_nn(pair, transfer[2 * q : 2 * q + 2].reshape(128, 64)).astype(BF))
        if q % 2:
            a, b = parents[q - 1], parents[q]
            row[0, gy * TD + q // 2] = jnp.concatenate([a, b], axis=1)
            row[1, gy * TD + q // 2] = jnp.concatenate([b, a], axis=1)

    pl.semaphore_wait(barrier, 6)

    def slot(dy, dz, part):
        start, size = SPAN[part]
        origin = ((z + (NZ - dz)) % NZ) * NY + (y + (NY - dy)) % NY
        return row.at[0, pl.ds(origin * TD + start, size)]

    def send(src, m, direction):
        part = m[2]
        ref = slot(src[0], src[1], part)
        pltpu.make_async_remote_copy(
            src_ref=ref, dst_ref=ref, send_sem=send_sem, recv_sem=recv_sem.at[NUMBER[m]],
            device_id=ids[direction], device_id_type=MESH,
        ).start()

    def receive(m):
        ref = slot(*m)
        pltpu.make_async_remote_copy(
            src_ref=ref, dst_ref=ref, send_sem=send_sem, recv_sem=recv_sem.at[NUMBER[m]],
            device_id=ids["y+"], device_id_type=MESH,
        ).wait_recv()

    for d, dy, dz, part in (
        ("y+", 1, 0, "A"), ("y-", -1, 0, "A"), ("z+", 0, 1, "B"), ("z-", 0, -1, "B"),
        ("y+", 1, 0, "B"), ("y-", -1, 0, "B"), ("z+", 0, 1, "A"), ("z-", 0, -1, "A"),
    ):
        send((0, 0), (dy, dz, part), d)

    own = win.at[0, pl.ds(mine, QD)]
    rims = [
        pltpu.make_async_remote_copy(
            src_ref=s, dst_ref=d, send_sem=rim_send.at[i], recv_sem=rim_recv.at[i],
            device_id=to, device_id_type=MESH,
        )
        for i, (s, d, to) in enumerate(
            [
                (own, own, nxt_id),
                (own, own, prv_id),
                (live.at[pl.ds(QD, 1)], live.at[pl.ds(0, 1)], nxt_id),
                (live.at[pl.ds(1, 1)], live.at[pl.ds(QD + 1, 1)], prv_id),
            ]
        )
    ]
    for rim in rims:
        rim.start()

    def do_diag(q):
        b0, b1 = basis[2 * q], basis[2 * q + 1]
        o = jnp.zeros((64, 64), BF)
        bdiag[q, :64] = jnp.concatenate([b0, o], axis=1)
        bdiag[q, 64:] = jnp.concatenate([o, b1], axis=1)

    def do_near(q):
        o = jnp.zeros((64, 64), BF)
        o2 = jnp.zeros((64, 128), BF)
        top = jnp.concatenate([o, nb[2 * q, 0], nb[2 * q, 1], nb[2 * q, 2], o2], axis=1)
        low_rows = jnp.concatenate(
            [o2, nb[2 * q + 1, 0], nb[2 * q + 1, 1], nb[2 * q + 1, 2], o], axis=1
        )
        lhs = jnp.concatenate([live[q], live[q + 1], live[q + 2]], axis=1)
        near[q] = dot_nt(lhs, jnp.concatenate([top, low_rows], axis=0))

    def do_couple(q):
        for i in range(8):
            cpl[q, :, 128 * i : 128 * i + 128] = jnp.concatenate(
                [pc[q, 2 * i], pc[q, 2 * i + 1]], axis=1
            )

    def pick(ref, p, q):
        tiles = ref.shape[1]
        a = ref[p & 1, (p >> 1) & (tiles - 1)]
        b = ref[1 - (q & 1), (q >> 1) & (tiles - 1)]
        return jnp.where(low, a, b)

    def leaf_sum(g):
        lhs = jnp.concatenate(
            [pick(win, lp[2 * i, g], lp[2 * i + 1, g]) for i in range(8)], axis=1
        )
        rhs = jnp.concatenate([lc[g, j] for j in range(16)], axis=1)
        return dot_nt(lhs, rhs)

    def do_far(q):
        far[q] = jnp.concatenate([leaf_sum(2 * q), leaf_sum(2 * q + 1)], axis=1)

    def take_rims():
        for rim in rims:
            rim.wait_recv()
        live[0] = jnp.where(dev > 0, live[0], zero)
        live[QD + 1] = jnp.where(dev < total - 1, live[QD + 1], zero)

        @pl.loop(0, QD)
        def _(t):
            win[1, before + t] = swap(win[0, before + t])
            win[1, after + t] = swap(win[0, after + t])

    def wait_load(i):
        return loads[i].wait

    work = [lambda q=q: do_diag(q) for q in range(QD)]
    work += [wait_load(4)] + [lambda q=q: do_near(q) for q in range(1, QD - 1)]
    work += [wait_load(8)] + [lambda q=q: do_couple(q) for q in range(QD)]
    work += [wait_load(5), wait_load(7), take_rims]
    work += [lambda: do_near(0), lambda: do_near(QD - 1)]
    work += [lambda q=q: do_far(q) for q in range(QD)]
    done = 0
    for s, step in enumerate(STEPS):
        for m in step:
            receive(m)
        dy, dz, part = step[0]
        for d, ny, nz, np_ in children(dy, dz, part[0] if len(step) == 2 else part):
            send((dy, dz), (ny, nz, np_), d)
        upto = min(len(work), (s + 1) * len(work) // (len(STEPS) - 6))
        for unit in work[done:upto]:
            unit()
        done = upto
        for m in step:
            start, size = SPAN[m[2]]
            origin = ((z + (NZ - dz)) % NZ) * NY + (y + (NY - dy)) % NY
            for t in range(size):
                at = origin * TD + start + t
                row[1, at] = swap(row[0, at])

    loads[6].wait()
    for q in range(QD):
        lhs = jnp.concatenate(
            [pick(row, pp[q, 2 * i], pp[q, 2 * i + 1]) for i in range(8)], axis=1
        )
        parent_far = dot_nt(lhs, cpl[q]).astype(BF)
        local = dot_nt(parent_far, transfer[2 * q : 2 * q + 2].reshape(128, 64)) + far[q]
        total_q = dot_nt(local.astype(BF), bdiag[q]) + near[q]
        m0, m1 = masks(q)
        out_ref[:, 128 * q : 128 * q + 128] = jnp.where(m0 | m1, total_q, 0.0).astype(BF)

    for rim in rims:
        rim.wait_send()
    sent = row.at[0, pl.ds(0, ROW_TILES - TD)]
    pltpu.make_async_remote_copy(
        src_ref=sent, dst_ref=sent, send_sem=send_sem, recv_sem=recv_sem.at[0],
        device_id=ids["y+"], device_id_type=MESH,
    ).wait_send()


def per_device(
    charges, panel_counts, basis, transfer, leaf_coupling, leaf_partners, near_blocks,
    parent_coupling, parent_partners,
):
    n = charges.shape[0]
    result = pl.pallas_call(
        kernel,
        out_shape=jax.ShapeDtypeStruct((R, n), BF),
        in_specs=[pl.BlockSpec(memory_space=pltpu.HBM)] * 9,
        out_specs=pl.BlockSpec(memory_space=pltpu.VMEM),
        scratch_shapes=[
            pltpu.VMEM((R, n), BF),
            pltpu.VMEM(basis.shape, BF),
            pltpu.VMEM(transfer.shape, BF),
            pltpu.VMEM(leaf_coupling.shape, BF),
            pltpu.VMEM(near_blocks.shape, BF),
            pltpu.VMEM(parent_coupling.shape, BF),
            pltpu.SMEM((LD,), jnp.int32),
            pltpu.SMEM((16, LD), jnp.int32),
            pltpu.SMEM((QD, 16), jnp.int32),
            pltpu.VMEM((QD + 2, R, 128), BF),
            pltpu.VMEM((2, WIN * QD, R, 128), BF),
            pltpu.VMEM((2, ROW_TILES, R, 128), BF),
            pltpu.VMEM((QD, 64, 1024), BF),
            pltpu.VMEM((QD, 128, 128), BF),
            pltpu.VMEM((QD, R, 128), F32),
            pltpu.VMEM((QD, R, 128), F32),
            pltpu.SemaphoreType.DMA((9,)),
            pltpu.SemaphoreType.DMA((len(MESSAGES),)),
            pltpu.SemaphoreType.DMA,
            pltpu.SemaphoreType.DMA((4,)),
            pltpu.SemaphoreType.DMA((4,)),
        ],
        compiler_params=pltpu.CompilerParams(
            collective_id=0, has_side_effects=True, vmem_limit_bytes=56 * 1024 * 1024
        ),
    )(
        charges.T, panel_counts, basis, transfer, leaf_coupling, leaf_partners.T, near_blocks,
        parent_coupling, parent_partners,
    )
    return result.T


def solution(mesh):
    in_specs = (
        P(("gx", "gy"), None),
        P(("gx", "gy")),
        P(("gx", "gy"), None, None),
        P(("gx", "gy"), None, None),
        P(("gx", "gy"), None, None, None),
        P(("gx", "gy"), None),
        P(("gx", "gy"), None, None, None),
        P(("gx", "gy"), None, None, None),
        P(("gx", "gy"), None),
    )
    out_specs = P(("gx", "gy"), None)
    return jax.shard_map(
        per_device, mesh=mesh, in_specs=in_specs, out_specs=out_specs, check_vma=False
    )
```

time: 118 us -> 42.2 us (0.36); the launches traced: 117 us -> 42.1 us
  waiting for transfers between devices: 67 us -> 0 us
  Pallas kernels: 0 us -> 40.5 us
  matrix products: 18.4 us -> 0 us
  between operations: 13.6 us -> 0.01 us
  local copies, waits for them, and re-layouts: 10.8 us -> 1.57 us
  starting transfers between devices: 6.02 us -> 0 us
    all_gather x1 -> x0, waiting for transfers between devices: 63.7 us -> none  [per_device(): row_coef = lax.all_gather(parent_coef, 'gy', axis=0, tiled=True)]
    pallas_call x0 -> x1, Pallas kernels: none -> 40.5 us  [per_device(): pl.pallas_call(kernel, out_shape=jax.ShapeDtypeStruct((R, n), BF), in_spe...]
    dot_general x8 -> x0, matrix products: 18.4 us -> none  [the longest x1 7.2 us: per_device(): jnp.einsum('gpk,gkr->gpr', basis, local_coef, preferred_element_type=jnp....]
    gather x2 -> x0, local copies, waits for them, and re-layouts: 6.72 us -> none  [the longest x1 3.54 us: per_device(): picked = window_coef[relative + leaves]]
    ppermute x2 -> x0, starting transfers between devices: 6.01 us -> none  [shifted(): return lax.ppermute(array, axis, pairs)]
    reshape x5 -> x0, local copies, waits for them, and re-layouts: 3.49 us -> none  [the longest x1 1.18 us: per_device(): live = charges.reshape(leaves, leaf_size, sides) * mask]
    ppermute x2 -> x0, waiting for transfers between devices: 3.26 us -> none  [shifted(): return lax.ppermute(array, axis, pairs)]
    unnamed x8 -> x1, local copies, waits for them, and re-layouts: 0.02 us -> 1.57 us
  transfers between devices with their start and end apart: 3 -> 0, of which waited for: 2 -> 0; matrix products, arithmetic and copies ran while one was open for 9% -> 0% of each run, Pallas kernels for 0% -> 0%
where the time goes in v1:
time: 42.2 us; the launch traced here: 42.1 us
  Pallas kernels  40.5 us (96%)
  local copies, waits for them, and re-layouts  1.57 us (4%)
    pallas_call x1, Pallas kernels, per_device(): pl.pallas_call(kernel, out_shape=jax.ShapeDtypeStruct((R, n), BF), in_spe...  40.5 us
    unnamed x1, local copies, waits for them, and re-layouts  1.57 us

profile of v1, /device:TPU:8, one launch (start us, length us, event | category | flops | bytes accessed | tf_op | source)
XLA Modules:
  0.0 42.1 jit_solution(5493302920592433020)
XLA Ops:
  0.0 40.5 %shard_map.91 = bf16[32,2048]{1,0:T(8,128)(2,1)} custom-call(bf16[32,2048]{1,0:T(8,128)(2,1)} %bitcast.4, s32[32]{0:T(128)} %cnt_hbm.1, bf16[32,64,64]{2,1,0:T(8,128)(2,1)} %basis_hbm.1, bf16[32,64,64]{2,1,0:T(8,128)(2,1)} %transfer_hbm.1, bf16[32,16,64,64]{3,2,1,0:T(8,128)(2,1)} %lc_hbm.1, s32[16,32]{1,0:T(8,128)} %bitcast.5, ...), custom_call_target="tpu_custom_call" | custom-call | tf_op jit(solution)/shard_map/pallas_call | solution.py:316
  40.5 1.6 %copy.11 = bf16[2048,32]{0,1:T(8,128)(2,1)} copy(bf16[2048,32]{0,1:T(8,128)(2,1)} %bitcast.3) | data formatting | bytes 262144

commit v2 on v1

v2 whole, which is shorter than its diff:
```python
import jax
import jax.numpy as jnp
from jax import lax
from jax.experimental import pallas as pl
from jax.experimental.pallas import tpu as pltpu
from jax.sharding import PartitionSpec as P

BF = jnp.bfloat16
F32 = jnp.float32
MESH = pl.DeviceIdType.MESH

NY = 4
NZ = 8
NGX = 8
NGY = NY * NZ
LD = 32
QD = 16
UD = QD
ROW_UNITS = NGY * UD
R = 32
WIN = 4

SPAN = {"A": (0, 6), "A0": (0, 3), "A1": (3, 3), "B": (6, 10), "B0": (6, 5), "B1": (11, 5)}

ROUTES = {
    (0, 0, "A"): (
        ("y+", 2, (2, 0, "A0")),
        ("y-", 2, (2, 0, "A1")),
        ("y+", 1, (1, 0, "A")),
        ("y-", 1, (-1, 0, "A")),
        ("z+", 1, (0, 1, "A")),
        ("z-", 1, (0, -1, "A")),
    ),
    (0, 0, "B"): (
        ("z+", 2, (0, 2, "B")),
        ("z+", 1, (0, 1, "B")),
        ("z-", 2, (0, -2, "B")),
        ("z-", 1, (0, -1, "B")),
        ("y+", 1, (1, 0, "B")),
        ("y-", 1, (-1, 0, "B")),
    ),
    (0, 1, "A"): (
        ("z+", 1, (0, 2, "A")),
    ),
    (0, -1, "A"): (
        ("z-", 1, (0, -2, "A")),
    ),
    (1, 0, "A"): (
        ("z+", 1, (1, 1, "A")),
        ("z-", 1, (1, -1, "A")),
    ),
    (-1, 0, "A"): (
        ("z+", 1, (-1, 1, "A")),
        ("z-", 1, (-1, -1, "A")),
    ),
    (1, 0, "B"): (
        ("y+", 1, (2, 0, "B0")),
    ),
    (-1, 0, "B"): (
        ("y-", 1, (2, 0, "B1")),
    ),
    (0, 1, "B"): (
        ("y+", 1, (1, 1, "B")),
        ("y-", 1, (-1, 1, "B")),
    ),
    (0, -1, "B"): (
        ("y+", 1, (1, -1, "B")),
        ("y-", 1, (-1, -1, "B")),
    ),
    (0, 2, "B"): (
        ("z+", 1, (0, 3, "B")),
        ("y+", 1, (1, 2, "B")),
        ("y-", 1, (-1, 2, "B")),
    ),
    (0, -2, "B"): (
        ("z-", 1, (0, -3, "B")),
        ("y+", 1, (1, -2, "B")),
        ("y-", 1, (-1, -2, "B")),
    ),
    (0, 2, "A"): (
        ("z+", 2, (0, 4, "A0")),
        ("z+", 1, (0, 3, "A")),
    ),
    (0, -2, "A"): (
        ("z-", 2, (0, 4, "A1")),
        ("z-", 1, (0, -3, "A")),
    ),
    (1, 1, "A"): (
        ("z+", 1, (1, 2, "A")),
    ),
    (1, -1, "A"): (
        ("z-", 1, (1, -2, "A")),
    ),
    (2, 0, "A"): (
        ("z+", 1, (2, 1, "A")),
        ("z-", 1, (2, -1, "A")),
    ),
    (-1, 1, "A"): (
        ("z+", 1, (-1, 2, "A")),
    ),
    (-1, -1, "A"): (
        ("z-", 1, (-1, -2, "A")),
    ),
    (0, 3, "B"): (
        ("z+", 1, (0, 4, "B0")),
        ("y+", 1, (1, 3, "B")),
        ("y-", 1, (-1, 3, "B")),
    ),
    (1, 1, "B"): (
        ("y+", 1, (2, 1, "B0")),
    ),
    (-1, 1, "B"): (
        ("y-", 1, (2, 1, "B1")),
    ),
    (0, -3, "B"): (
        ("z-", 1, (0, 4, "B1")),
        ("y+", 1, (1, -3, "B")),
        ("y-", 1, (-1, -3, "B")),
    ),
    (1, -1, "B"): (
        ("y+", 1, (2, -1, "B0")),
    ),
    (-1, -1, "B"): (
        ("y-", 1, (2, -1, "B1")),
    ),
    (1, 2, "A"): (
        ("z+", 2, (1, 4, "A0")),
        ("z+", 1, (1, 3, "A")),
    ),
    (1, -2, "A"): (
        ("z-", 2, (1, 4, "A1")),
        ("z-", 1, (1, -3, "A")),
    ),
    (1, 2, "B"): (
        ("y+", 1, (2, 2, "B0")),
    ),
    (-1, 2, "B"): (
        ("y-", 1, (2, 2, "B1")),
    ),
    (2, -1, "A"): (
        ("z-", 1, (2, -2, "A")),
    ),
    (2, 1, "A"): (
        ("z+", 1, (2, 2, "A")),
    ),
    (-1, 2, "A"): (
        ("z+", 2, (-1, 4, "A0")),
        ("z+", 1, (-1, 3, "A")),
    ),
    (1, -2, "B"): (
        ("y+", 1, (2, -2, "B0")),
    ),
    (-1, -2, "B"): (
        ("y-", 1, (2, -2, "B1")),
    ),
    (-1, -2, "A"): (
        ("z-", 2, (-1, 4, "A1")),
        ("z-", 1, (-1, -3, "A")),
    ),
    (0, 4, "B"): (
        ("y+", 2, (2, 4, "B0")),
        ("y-", 2, (2, 4, "B1")),
        ("y+", 1, (1, 4, "B")),
        ("y-", 1, (-1, 4, "B")),
    ),
    (1, 3, "B"): (
        ("y+", 1, (2, 3, "B0")),
    ),
    (-1, 3, "B"): (
        ("y-", 1, (2, 3, "B1")),
    ),
    (2, -2, "A"): (
        ("z-", 2, (2, 4, "A1")),
        ("z-", 1, (2, -3, "A")),
    ),
    (2, 2, "A"): (
        ("z+", 2, (2, 4, "A0")),
        ("z+", 1, (2, 3, "A")),
    ),
    (1, -3, "B"): (
        ("y+", 1, (2, -3, "B0")),
    ),
    (-1, -3, "B"): (
        ("y-", 1, (2, -3, "B1")),
    ),
}

FIRST_WORK = 50
STEPS = (
    (((0, 1, "A"),), 0),
    (((0, -1, "A"),), 0),
    (((1, 0, "A"),), 0),
    (((-1, 0, "A"),), 0),
    (((1, 0, "B"),), 0),
    (((-1, 0, "B"),), 0),
    (((0, 1, "B"),), 0),
    (((0, -1, "B"),), 0),
    (((0, 2, "B"),), 0),
    (((0, -2, "B"),), 0),
    (((0, 2, "A"),), 0),
    (((0, -2, "A"),), 0),
    (((1, 1, "A"),), 0),
    (((1, -1, "A"),), 0),
    (((2, 0, "A0"), (2, 0, "A1")), 0),
    (((-1, 1, "A"),), 0),
    (((-1, -1, "A"),), 1),
    (((2, 0, "B0"), (2, 0, "B1")), 7),
    (((0, 3, "B"),), 0),
    (((1, 1, "B"),), 0),
    (((-1, 1, "B"),), 0),
    (((0, -3, "B"),), 3),
    (((0, 3, "A"),), 0),
    (((1, -1, "B"),), 0),
    (((0, -3, "A"),), 0),
    (((-1, -1, "B"),), 2),
    (((1, 2, "A"),), 0),
    (((1, -2, "A"),), 2),
    (((1, 2, "B"),), 0),
    (((-1, 2, "B"),), 0),
    (((2, -1, "A"),), 0),
    (((2, 1, "A"),), 1),
    (((0, 4, "A0"), (0, 4, "A1")), 3),
    (((-1, 2, "A"),), 0),
    (((1, -2, "B"),), 0),
    (((-1, -2, "B"),), 0),
    (((-1, -2, "A"),), 0),
    (((0, 4, "B0"), (0, 4, "B1")), 0),
    (((1, 3, "B"),), 0),
    (((-1, 3, "B"),), 0),
    (((2, 1, "B0"), (2, 1, "B1")), 0),
    (((1, 3, "A"),), 0),
    (((1, -3, "A"),), 0),
    (((2, -2, "A"),), 0),
    (((2, 2, "A"),), 0),
    (((1, -3, "B"),), 0),
    (((-1, -3, "B"),), 0),
    (((1, 4, "A0"), (1, 4, "A1")), 0),
    (((2, -1, "B0"), (2, -1, "B1")), 0),
    (((-1, 3, "A"),), 0),
    (((-1, -3, "A"),), 0),
    (((2, 2, "B0"), (2, 2, "B1")), 0),
    (((-1, 4, "A0"), (-1, 4, "A1")), 0),
    (((2, -2, "B0"), (2, -2, "B1")), 0),
    (((2, -3, "A"),), 0),
    (((1, 4, "B"),), 0),
    (((-1, 4, "B"),), 0),
    (((2, 3, "A"),), 0),
    (((2, 4, "A0"), (2, 4, "A1")), 0),
    (((2, 3, "B0"), (2, 3, "B1")), 0),
    (((2, 4, "B0"), (2, 4, "B1")), 0),
    (((2, -3, "B0"), (2, -3, "B1")), 0),
)
MESSAGES = tuple(m for step, _ in STEPS for m in step)
REACH = tuple(sorted({(d[0], h * (1 if d[1] == "+" else -1) % (NY if d[0] == "y" else NZ)) for out in ROUTES.values() for d, h, _ in out}))
NUMBER = {m: i for i, m in enumerate(MESSAGES)}


def dot_nn(a, b):
    return lax.dot_general(a, b, (((1,), (0,)), ((), ())), preferred_element_type=F32)


def dot_nt(a, b):
    return lax.dot_general(a, b, (((1,), (1,)), ((), ())), preferred_element_type=F32)


def kernel(
    ch_hbm, cnt_hbm, basis_hbm, transfer_hbm, lc_hbm, lp_hbm, nb_hbm, pc_hbm, pp_hbm,
    out_ref,
    ch, basis, transfer, lc, nb, pc, cnt, lp, pp,
    live, win, row, cpl, bdiag, near, far, held, coefs,
    in_sem, recv_sem, send_sem, rim_recv, rim_send,
):
    gx = lax.axis_index("gx")
    gy = lax.axis_index("gy")
    z = gy // NY
    y = gy % NY
    dev = gx * NGY + gy
    total = NGX * NGY
    prv = (dev + total - 1) % total
    nxt = (dev + 1) % total
    prv_id = (prv // NGY, prv % NGY)
    nxt_id = (nxt // NGY, nxt % NGY)

    def reach(axis, steps):
        if axis == "y":
            return gx, z * NY + (y + steps) % NY
        return gx, ((z + steps) % NZ) * NY + y


    loads = [
        pltpu.make_async_copy(s, d, in_sem.at[i])
        for i, (s, d) in enumerate(
            [
                (ch_hbm, ch), (cnt_hbm, cnt), (basis_hbm, basis), (transfer_hbm, transfer),
                (nb_hbm, nb), (lp_hbm, lp), (pp_hbm, pp), (pc_hbm, pc), (lc_hbm, lc),
            ]
        )
    ]
    for load in loads:
        load.start()

    barrier = pltpu.get_barrier_semaphore()
    greeted = [reach(axis, steps) for axis, steps in REACH] + [prv_id, nxt_id]
    for d in greeted:
        pl.semaphore_signal(barrier, inc=1, device_id=d, device_id_type=MESH)

    mine, before, after = ((d % WIN) * QD for d in (dev, prv, nxt))

    lane = lax.broadcasted_iota(jnp.int32, (R, 128), 1)
    low = lane < 64

    def masks(q):
        return lane < cnt[2 * q], (lane >= 64) & (lane < cnt[2 * q + 1] + 64)

    def swap(tile):
        return jnp.concatenate([tile[:, 64:], tile[:, :64]], axis=1)

    for load in loads[:4]:
        load.wait()

    zero = jnp.zeros((R, 128), BF)
    parents = []
    for q in range(QD):
        m0, m1 = masks(q)
        tile = ch[:, 128 * q : 128 * q + 128]
        l0 = jnp.where(m0, tile, zero)
        l1 = jnp.where(m1, tile, zero)
        live[q + 1] = l0 + l1
        coef = dot_nn(jnp.concatenate([l0, l1], axis=0), basis[2 * q : 2 * q + 2].reshape(128, 64))
        coef = coef.astype(BF)
        pair = jnp.concatenate([coef[:R], coef[R:]], axis=1)
        win[0, mine + q] = pair
        win[1, mine + q] = jnp.concatenate([coef[R:], coef[:R]], axis=1)
        parents.append(dot_nn(pair, transfer[2 * q : 2 * q + 2].reshape(128, 64)).astype(BF))
        if q % 2:
            a, b = parents[q - 1], parents[q]
            at = pl.ds(gy * UD + q - 1, 2)
            row[0, at] = jnp.concatenate([a, b], axis=1).reshape(2, 16, 128)
            row[1, at] = jnp.concatenate([b, a], axis=1).reshape(2, 16, 128)

    pl.semaphore_wait(barrier, len(greeted))

    def rows_of(dy, dz, part):
        start, size = SPAN[part]
        origin = ((z + (NZ - dz)) % NZ) * NY + (y + (NY - dy)) % NY
        return pl.ds(origin * UD + start, size)

    def copy_of(rows, m, to):
        ref = row.at[0, rows]
        return pltpu.make_async_remote_copy(
            src_ref=ref, dst_ref=ref, send_sem=send_sem, recv_sem=recv_sem.at[NUMBER[m]],
            device_id=to, device_id_type=MESH,
        )

    def send_on(dy, dz, part):
        for d, steps, m in ROUTES.get((dy, dz, part), ()):
            steps = steps if d[1] == "+" else (NY if d[0] == "y" else NZ) - steps
            copy_of(rows_of(dy, dz, m[2]), m, reach(d[0], steps)).start()

    def receive(m):
        copy_of(rows_of(*m), m, greeted[0]).wait_recv()

    send_on(0, 0, "A")
    send_on(0, 0, "B")

    own = win.at[0, pl.ds(mine, QD)]
    rims = [
        pltpu.make_async_remote_copy(
            src_ref=s, dst_ref=d, send_sem=rim_send.at[i], recv_sem=rim_recv.at[i],
            device_id=to, device_id_type=MESH,
        )
        for i, (s, d, to) in enumerate(
            [
                (own, own, nxt_id),
                (own, own, prv_id),
                (live.at[pl.ds(QD, 1)], live.at[pl.ds(0, 1)], nxt_id),
                (live.at[pl.ds(1, 1)], live.at[pl.ds(QD + 1, 1)], prv_id),
            ]
        )
    ]
    for rim in rims:
        rim.start()

    def do_diag(q):
        b0, b1 = basis[2 * q], basis[2 * q + 1]
        o = jnp.zeros((64, 64), BF)
        bdiag[q, :64] = jnp.concatenate([b0, o], axis=1)
        bdiag[q, 64:] = jnp.concatenate([o, b1], axis=1)

    def do_near(q):
        o = jnp.zeros((64, 64), BF)
        o2 = jnp.zeros((64, 128), BF)
        top = jnp.concatenate([o, nb[2 * q, 0], nb[2 * q, 1], nb[2 * q, 2], o2], axis=1)
        low_rows = jnp.concatenate(
            [o2, nb[2 * q + 1, 0], nb[2 * q + 1, 1], nb[2 * q + 1, 2], o], axis=1
        )
        lhs = jnp.concatenate([live[q], live[q + 1], live[q + 2]], axis=1)
        near[q] = dot_nt(lhs, jnp.concatenate([top, low_rows], axis=0))

    def do_couple(q):
        for i in range(8):
            cpl[q, :, 128 * i : 128 * i + 128] = jnp.concatenate(
                [pc[q, 2 * i], pc[q, 2 * i + 1]], axis=1
            )

    def pick_leaves(p, q):
        a = win[p & 1, (p >> 1) & (WIN * QD - 1)]
        b = win[1 - (q & 1), (q >> 1) & (WIN * QD - 1)]
        return jnp.where(low, a, b)

    def pick_parents(p, q):
        a = (p >> 1) & (ROW_UNITS // 2 - 1)
        b = (q >> 1) & (ROW_UNITS // 2 - 1)
        return jnp.concatenate(
            [
                jnp.where(low[:16], row[p & 1, 2 * a + i], row[1 - (q & 1), 2 * b + i])
                for i in range(2)
            ],
            axis=0,
        )

    def leaf_sum(g):
        lhs = jnp.concatenate(
            [pick_leaves(lp[2 * i, g], lp[2 * i + 1, g]) for i in range(8)], axis=1
        )
        rhs = jnp.concatenate([lc[g, j] for j in range(16)], axis=1)
        return dot_nt(lhs, rhs)

    def do_far(q):
        far[q] = jnp.concatenate([leaf_sum(2 * q), leaf_sum(2 * q + 1)], axis=1)

    def take_rims():
        for rim in rims:
            rim.wait_recv()
        live[0] = jnp.where(dev > 0, live[0], zero)
        live[QD + 1] = jnp.where(dev < total - 1, live[QD + 1], zero)

        @pl.loop(0, QD)
        def _(t):
            win[1, before + t] = swap(win[0, before + t])
            win[1, after + t] = swap(win[0, after + t])

    def wait_load(i):
        return loads[i].wait

    work = [lambda q=q: do_diag(q) for q in range(QD)]
    work += [wait_load(4)] + [lambda q=q: do_near(q) for q in range(1, QD - 1)]
    work += [wait_load(7)] + [lambda q=q: do_couple(q) for q in range(QD)]
    work += [wait_load(5), wait_load(8), take_rims]
    work += [lambda: do_near(0), lambda: do_near(QD - 1)]
    work += [lambda q=q: do_far(q) for q in range(QD)]
    todo = iter(work)

    def do_work(n):
        for _ in range(n):
            next(todo, lambda: None)()

    do_work(FIRST_WORK)
    for step, pieces in STEPS:
        for m in step:
            receive(m)
        dy, dz, part = step[0]
        send_on(dy, dz, part[0] if len(step) == 2 else part)
        for m in step:
            rows = rows_of(*m)
            n = SPAN[m[2]][1]
            row[1, rows] = swap(row[0, rows].reshape(n * 16, 128)).reshape(n, 16, 128)
        do_work(pieces)
    for unit in todo:
        unit()

    loads[6].wait()
    for q in range(QD):
        lhs = jnp.concatenate(
            [pick_parents(pp[q, 2 * i], pp[q, 2 * i + 1]) for i in range(8)], axis=1
        )
        held[q] = dot_nt(lhs, cpl[q]).astype(BF)
    for q in range(QD):
        local = dot_nt(held[q], transfer[2 * q : 2 * q + 2].reshape(128, 64)) + far[q]
        coefs[q] = local.astype(BF)
    for q in range(QD):
        total_q = dot_nt(coefs[q], bdiag[q]) + near[q]
        m0, m1 = masks(q)
        out_ref[:, 128 * q : 128 * q + 128] = jnp.where(m0 | m1, total_q, 0.0).astype(BF)

    for rim in rims:
        rim.wait_send()
    copy_of(pl.ds(0, ROW_UNITS - UD), MESSAGES[0], greeted[0]).wait_send()


def per_device(
    charges, panel_counts, basis, transfer, leaf_coupling, leaf_partners, near_blocks,
    parent_coupling, parent_partners,
):
    n = charges.shape[0]
    result = pl.pallas_call(
        kernel,
        out_shape=jax.ShapeDtypeStruct((R, n), BF),
        in_specs=[pl.BlockSpec(memory_space=pltpu.HBM)] * 9,
        out_specs=pl.BlockSpec(memory_space=pltpu.VMEM),
        scratch_shapes=[
            pltpu.VMEM((R, n), BF),
            pltpu.VMEM(basis.shape, BF),
            pltpu.VMEM(transfer.shape, BF),
            pltpu.VMEM(leaf_coupling.shape, BF),
            pltpu.VMEM(near_blocks.shape, BF),
            pltpu.VMEM(parent_coupling.shape, BF),
            pltpu.SMEM((LD,), jnp.int32),
            pltpu.SMEM((16, LD), jnp.int32),
            pltpu.SMEM((QD, 16), jnp.int32),
            pltpu.VMEM((QD + 2, R, 128), BF),
            pltpu.VMEM((2, WIN * QD, R, 128), BF),
            pltpu.VMEM((2, ROW_UNITS, 16, 128), BF),
            pltpu.VMEM((QD, 64, 1024), BF),
            pltpu.VMEM((QD, 128, 128), BF),
            pltpu.VMEM((QD, R, 128), F32),
            pltpu.VMEM((QD, R, 128), F32),
            pltpu.VMEM((QD, R, 64), BF),
            pltpu.VMEM((QD, R, 128), BF),
            pltpu.SemaphoreType.DMA((9,)),
            pltpu.SemaphoreType.DMA((len(MESSAGES),)),
            pltpu.SemaphoreType.DMA,
            pltpu.SemaphoreType.DMA((4,)),
            pltpu.SemaphoreType.DMA((4,)),
        ],
        compiler_params=pltpu.CompilerParams(
            collective_id=0, has_side_effects=True, vmem_limit_bytes=56 * 1024 * 1024
        ),
    )(
        charges.T, panel_counts, basis, transfer, leaf_coupling, leaf_partners.T, near_blocks,
        parent_coupling, parent_partners,
    )
    return result.T


def solution(mesh):
    in_specs = (
        P(("gx", "gy"), None),
        P(("gx", "gy")),
        P(("gx", "gy"), None, None),
        P(("gx", "gy"), None, None),
        P(("gx", "gy"), None, None, None),
        P(("gx", "gy"), None),
        P(("gx", "gy"), None, None, None),
        P(("gx", "gy"), None, None, None),
        P(("gx", "gy"), None),
    )
    out_specs = P(("gx", "gy"), None)
    return jax.shard_map(
        per_device, mesh=mesh, in_specs=in_specs, out_specs=out_specs, check_vma=False
    )
```

time: 42.2 us -> 35.6 us (0.84)
  Pallas kernels: 40.5 us -> 33.8 us
    pallas_call x1, Pallas kernels: 40.5 us -> 33.8 us  [per_device(): pl.pallas_call(kernel, out_shape=jax.ShapeDtypeStruct((R, n), BF), in_spe...]
where the time goes in v2:
time: 35.6 us; the launch traced here: 35.4 us
  Pallas kernels  33.8 us (95%)
  local copies, waits for them, and re-layouts  1.57 us (4%)
    pallas_call x1, Pallas kernels, per_device(): pl.pallas_call(kernel, out_shape=jax.ShapeDtypeStruct((R, n), BF), in_spe...  33.8 us
    unnamed x1, local copies, waits for them, and re-layouts  1.57 us

profile of v2, /device:TPU:8, one launch (start us, length us, event | category | flops | bytes accessed | tf_op | source)
XLA Modules:
  0.0 35.4 jit_solution(1646979867657945238)
XLA Ops:
  0.0 33.8 %shard_map.91 = bf16[32,2048]{1,0:T(8,128)(2,1)} custom-call(bf16[32,2048]{1,0:T(8,128)(2,1)} %bitcast.4, s32[32]{0:T(128)} %cnt_hbm.1, bf16[32,64,64]{2,1,0:T(8,128)(2,1)} %basis_hbm.1, bf16[32,64,64]{2,1,0:T(8,128)(2,1)} %transfer_hbm.1, bf16[32,16,64,64]{3,2,1,0:T(8,128)(2,1)} %lc_hbm.1, s32[16,32]{1,0:T(8,128)} %bitcast.5, ...), custom_call_target="tpu_custom_call" | custom-call | tf_op jit(solution)/shard_map/pallas_call | solution.py:496
  33.9 1.6 %copy.11 = bf16[2048,32]{0,1:T(8,128)(2,1)} copy(bf16[2048,32]{0,1:T(8,128)(2,1)} %bitcast.3) | data formatting | bytes 262144

commit v3 on v2

--- a/solution.py
+++ b/solution.py
@@ -19,239 +19,143 @@
 ROW_UNITS = NGY * UD
 R = 32
 WIN = 4
-
-SPAN = {"A": (0, 6), "A0": (0, 3), "A1": (3, 3), "B": (6, 10), "B0": (6, 5), "B1": (11, 5)}
+RIM = 4
+
+SPAN = {"A": (0, 7), "A0": (0, 4), "A1": (4, 3), "B": (7, 9), "B0": (7, 5), "B1": (12, 4)}
+
+FIRST = (
+    ("z+", 2, (0, 2, "B")),
+    ("y+", 1, (1, 0, "B")),
+    ("y+", 2, (2, 0, "A0")),
+    ("z-", 2, (0, -2, "B")),
+    ("y-", 2, (2, 0, "A1")),
+    ("z-", 1, (0, -1, "B")),
+    ("z+", 1, (0, 1, "B")),
+    ("y-", 1, (-1, 0, "A")),
+    ("y-", 1, (-1, 0, "B")),
+    ("z+", 1, (0, 1, "A")),
+    ("z-", 1, (0, -1, "A")),
+    ("y+", 1, (1, 0, "A")),
+)
 
 ROUTES = {
-    (0, 0, "A"): (
-        ("y+", 2, (2, 0, "A0")),
-        ("y-", 2, (2, 0, "A1")),
-        ("y+", 1, (1, 0, "A")),
-        ("y-", 1, (-1, 0, "A")),
-        ("z+", 1, (0, 1, "A")),
-        ("z-", 1, (0, -1, "A")),
-    ),
-    (0, 0, "B"): (
-        ("z+", 2, (0, 2, "B")),
-        ("z+", 1, (0, 1, "B")),
-        ("z-", 2, (0, -2, "B")),
-        ("z-", 1, (0, -1, "B")),
-        ("y+", 1, (1, 0, "B")),
-        ("y-", 1, (-1, 0, "B")),
-    ),
-    (0, 1, "A"): (
-        ("z+", 1, (0, 2, "A")),
-    ),
-    (0, -1, "A"): (
-        ("z-", 1, (0, -2, "A")),
-    ),
-    (1, 0, "A"): (
-        ("z+", 1, (1, 1, "A")),
-        ("z-", 1, (1, -1, "A")),
-    ),
-    (-1, 0, "A"): (
-        ("z+", 1, (-1, 1, "A")),
-        ("z-", 1, (-1, -1, "A")),
-    ),
-    (1, 0, "B"): (
-        ("y+", 1, (2, 0, "B0")),
-    ),
-    (-1, 0, "B"): (
-        ("y-", 1, (2, 0, "B1")),
-    ),
-    (0, 1, "B"): (
-        ("y+", 1, (1, 1, "B")),
-        ("y-", 1, (-1, 1, "B")),
-    ),
-    (0, -1, "B"): (
-        ("y+", 1, (1, -1, "B")),
-        ("y-", 1, (-1, -1, "B")),
-    ),
-    (0, 2, "B"): (
-        ("z+", 1, (0, 3, "B")),
-        ("y+", 1, (1, 2, "B")),
-        ("y-", 1, (-1, 2, "B")),
-    ),
-    (0, -2, "B"): (
-        ("z-", 1, (0, -3, "B")),
-        ("y+", 1, (1, -2, "B")),
-        ("y-", 1, (-1, -2, "B")),
-    ),
-    (0, 2, "A"): (
-        ("z+", 2, (0, 4, "A0")),
-        ("z+", 1, (0, 3, "A")),
-    ),
-    (0, -2, "A"): (
-        ("z-", 2, (0, 4, "A1")),
-        ("z-", 1, (0, -3, "A")),
-    ),
-    (1, 1, "A"): (
-        ("z+", 1, (1, 2, "A")),
-    ),
-    (1, -1, "A"): (
-        ("z-", 1, (1, -2, "A")),
-    ),
-    (2, 0, "A"): (
-        ("z+", 1, (2, 1, "A")),
-        ("z-", 1, (2, -1, "A")),
-    ),
-    (-1, 1, "A"): (
-        ("z+", 1, (-1, 2, "A")),
-    ),
-    (-1, -1, "A"): (
-        ("z-", 1, (-1, -2, "A")),
-    ),
-    (0, 3, "B"): (
-        ("z+", 1, (0, 4, "B0")),
-        ("y+", 1, (1, 3, "B")),
-        ("y-", 1, (-1, 3, "B")),
-    ),
-    (1, 1, "B"): (
-        ("y+", 1, (2, 1, "B0")),
-    ),
-    (-1, 1, "B"): (
-        ("y-", 1, (2, 1, "B1")),
-    ),
-    (0, -3, "B"): (
-        ("z-", 1, (0, 4, "B1")),
-        ("y+", 1, (1, -3, "B")),
-        ("y-", 1, (-1, -3, "B")),
-    ),
-    (1, -1, "B"): (
-        ("y+", 1, (2, -1, "B0")),
-    ),
-    (-1, -1, "B"): (
-        ("y-", 1, (2, -1, "B1")),
-    ),
-    (1, 2, "A"): (
-        ("z+", 2, (1, 4, "A0")),
-        ("z+", 1, (1, 3, "A")),
-    ),
-    (1, -2, "A"): (
-        ("z-", 2, (1, 4, "A1")),
-        ("z-", 1, (1, -3, "A")),
-    ),
-    (1, 2, "B"): (
-        ("y+", 1, (2, 2, "B0")),
-    ),
-    (-1, 2, "B"): (
-        ("y-", 1, (2, 2, "B1")),
-    ),
-    (2, -1, "A"): (
-        ("z-", 1, (2, -2, "A")),
-    ),
-    (2, 1, "A"): (
-        ("z+", 1, (2, 2, "A")),
-    ),
-    (-1, 2, "A"): (
-        ("z+", 2, (-1, 4, "A0")),
-        ("z+", 1, (-1, 3, "A")),
-    ),
-    (1, -2, "B"): (
-        ("y+", 1, (2, -2, "B0")),
-    ),
-    (-1, -2, "B"): (
-        ("y-", 1, (2, -2, "B1")),
-    ),
-    (-1, -2, "A"): (
-        ("z-", 2, (-1, 4, "A1")),
-        ("z-", 1, (-1, -3, "A")),
-    ),
-    (0, 4, "B"): (
-        ("y+", 2, (2, 4, "B0")),
-        ("y-", 2, (2, 4, "B1")),
-        ("y+", 1, (1, 4, "B")),
-        ("y-", 1, (-1, 4, "B")),
-    ),
-    (1, 3, "B"): (
-        ("y+", 1, (2, 3, "B0")),
-    ),
-    (-1, 3, "B"): (
-        ("y-", 1, (2, 3, "B1")),
-    ),
-    (2, -2, "A"): (
-        ("z-", 2, (2, 4, "A1")),
-        ("z-", 1, (2, -3, "A")),
-    ),
-    (2, 2, "A"): (
-        ("z+", 2, (2, 4, "A0")),
-        ("z+", 1, (2, 3, "A")),
-    ),
-    (1, -3, "B"): (
-        ("y+", 1, (2, -3, "B0")),
-    ),
-    (-1, -3, "B"): (
-        ("y-", 1, (2, -3, "B1")),
-    ),
+    (1, 0, "B"): (("y+", 1, (2, 0, "B0")),),
+    (-1, 0, "A"): (("z+", 1, (-1, 1, "A")), ("z-", 1, (-1, -1, "A"))),
+    (0, 1, "B"): (("y+", 1, (1, 1, "B")), ("y-", 1, (-1, 1, "B"))),
+    (0, -1, "B"): (("y+", 1, (1, -1, "B")), ("y-", 1, (-1, -1, "B"))),
+    (1, 0, "A"): (("z+", 1, (1, 1, "A")), ("z-", 1, (1, -1, "A"))),
+    (-1, 0, "B"): (("y-", 1, (2, 0, "B1")),),
+    (0, 1, "A"): (("z+", 1, (0, 2, "A")),),
+    (0, -1, "A"): (("z-", 1, (0, -2, "A")),),
+    (0, 2, "B"): (("z+", 1, (0, 3, "B")), ("y+", 1, (1, 2, "B")), ("y-", 1, (-1, 2, "B"))),
+    (0, -2, "B"): (("z-", 1, (0, -3, "B")), ("y+", 1, (1, -2, "B")), ("y-", 1, (-1, -2, "B"))),
+    (2, 0, "A"): (("z+", 1, (2, 1, "A")), ("z-", 1, (2, -1, "A"))),
+    (-1, 1, "A"): (("z+", 1, (-1, 2, "A")),),
+    (-1, -1, "A"): (("z-", 1, (-1, -2, "A")),),
+    (-1, 1, "B"): (("y-", 1, (2, 1, "B1")),),
+    (1, 1, "B"): (("y+", 1, (2, 1, "B0")),),
+    (1, 1, "A"): (("z+", 1, (1, 2, "A")),),
+    (1, -1, "A"): (("z-", 1, (1, -2, "A")),),
+    (0, 2, "A"): (("z+", 1, (0, 3, "A")),),
+    (-1, -1, "B"): (("y-", 1, (2, -1, "B1")),),
+    (1, -1, "B"): (("y+", 1, (2, -1, "B0")),),
+    (0, -2, "A"): (("z-", 1, (0, -3, "A")),),
+    (0, 3, "B"): (("z+", 1, (0, 4, "B0")), ("y+", 1, (1, 3, "B")), ("y-", 1, (-1, 3, "B"))),
+    (1, 2, "B"): (("y+", 1, (2, 2, "B0")),),
+    (0, -3, "B"): (("z-", 1, (0, 4, "B1")), ("y+", 1, (1, -3, "B")), ("y-", 1, (-1, -3, "B"))),
+    (-1, 2, "B"): (("y-", 1, (2, 2, "B1")),),
+    (2, 1, "A"): (("z+", 1, (2, 2, "A")),),
+    (2, -1, "A"): (("z-", 1, (2, -2, "A")),),
+    (1, -2, "B"): (("y+", 1, (2, -2, "B0")),),
+    (-1, -2, "B"): (("y-", 1, (2, -2, "B1")),),
+    (-1, 2, "A"): (("z+", 1, (-1, 3, "A")),),
+    (-1, -2, "A"): (("z-", 1, (-1, -3, "A")),),
+    (1, 2, "A"): (("z+", 1, (1, 3, "A")),),
+    (1, -2, "A"): (("z-", 1, (1, -3, "A")),),
+    (0, 3, "A"): (("z+", 1, (0, 4, "A0")),),
+    (0, -3, "A"): (("z-", 1, (0, 4, "A1")),),
+    (1, 3, "B"): (("y+", 1, (2, 3, "B0")),),
+    (0, 4, "B"): (("y+", 2, (2, 4, "B0")), ("y-", 2, (2, 4, "B1")), ("y+", 1, (1, 4, "B")), ("y-", 1, (-1, 4, "B"))),
+    (-1, 3, "B"): (("y-", 1, (2, 3, "B1")),),
+    (2, 2, "A"): (("z+", 2, (2, 4, "A0")), ("z+", 1, (2, 3, "A"))),
+    (2, -2, "A"): (("z-", 2, (2, 4, "A1")), ("z-", 1, (2, -3, "A"))),
+    (-1, 3, "A"): (("z+", 1, (-1, 4, "A0")),),
+    (-1, -3, "A"): (("z-", 1, (-1, 4, "A1")),),
+    (-1, -3, "B"): (("y-", 1, (2, -3, "B1")),),
+    (1, -3, "B"): (("y+", 1, (2, -3, "B0")),),
+    (1, 3, "A"): (("z+", 1, (1, 4, "A0")),),
+    (1, -3, "A"): (("z-", 1, (1, 4, "A1")),),
 }
 
+RIM_AT = (-1, -1, 12, 22)
 FIRST_WORK = 50
 STEPS = (
+    (((1, 0, "B"),), 0),
+    (((-1, 0, "A"),), 0),
+    (((0, 1, "B"),), 0),
+    (((0, -1, "B"),), 0),
+    (((1, 0, "A"),), 0),
+    (((-1, 0, "B"),), 0),
     (((0, 1, "A"),), 0),
     (((0, -1, "A"),), 0),
-    (((1, 0, "A"),), 0),
-    (((-1, 0, "A"),), 0),
-    (((1, 0, "B"),), 0),
-    (((-1, 0, "B"),), 0),
-    (((0, 1, "B"),), 0),
-    (((0, -1, "B"),), 0),
     (((0, 2, "B"),), 0),
     (((0, -2, "B"),), 0),
-    (((0, 2, "A"),), 0),
-    (((0, -2, "A"),), 0),
+    (((2, 0, "A0"), (2, 0, "A1")), 0),
+    (((-1, 1, "A"),), 0),
+    (((-1, -1, "A"),), 0),
+    (((-1, 1, "B"),), 0),
+    (((1, 1, "B"),), 0),
     (((1, 1, "A"),), 0),
     (((1, -1, "A"),), 0),
-    (((2, 0, "A0"), (2, 0, "A1")), 0),
-    (((-1, 1, "A"),), 0),
-    (((-1, -1, "A"),), 1),
-    (((2, 0, "B0"), (2, 0, "B1")), 7),
+    (((0, 2, "A"),), 0),
+    (((-1, -1, "B"),), 0),
+    (((1, -1, "B"),), 0),
+    (((0, -2, "A"),), 0),
+    (((2, 0, "B0"), (2, 0, "B1")), 0),
     (((0, 3, "B"),), 0),
-    (((1, 1, "B"),), 0),
-    (((-1, 1, "B"),), 0),
-    (((0, -3, "B"),), 3),
-    (((0, 3, "A"),), 0),
-    (((1, -1, "B"),), 0),
-    (((0, -3, "A"),), 0),
-    (((-1, -1, "B"),), 2),
-    (((1, 2, "A"),), 0),
-    (((1, -2, "A"),), 2),
     (((1, 2, "B"),), 0),
+    (((0, -3, "B"),), 0),
     (((-1, 2, "B"),), 0),
+    (((2, 1, "A"),), 0),
     (((2, -1, "A"),), 0),
-    (((2, 1, "A"),), 1),
-    (((0, 4, "A0"), (0, 4, "A1")), 3),
-    (((-1, 2, "A"),), 0),
     (((1, -2, "B"),), 0),
     (((-1, -2, "B"),), 0),
+    (((-1, 2, "A"),), 0),
     (((-1, -2, "A"),), 0),
+    (((1, 2, "A"),), 0),
+    (((1, -2, "A"),), 0),
+    (((2, 1, "B0"), (2, 1, "B1")), 0),
+    (((2, -1, "B0"), (2, -1, "B1")), 0),
+    (((0, 3, "A"),), 0),
+    (((0, -3, "A"),), 0),
+    (((1, 3, "B"),), 0),
     (((0, 4, "B0"), (0, 4, "B1")), 0),
-    (((1, 3, "B"),), 0),
     (((-1, 3, "B"),), 0),
-    (((2, 1, "B0"), (2, 1, "B1")), 0),
+    (((2, 2, "A"),), 0),
+    (((2, -2, "A"),), 8),
+    (((-1, 3, "A"),), 0),
+    (((-1, -3, "A"),), 0),
+    (((-1, -3, "B"),), 0),
+    (((1, -3, "B"),), 0),
+    (((2, 2, "B0"), (2, 2, "B1")), 1),
     (((1, 3, "A"),), 0),
     (((1, -3, "A"),), 0),
-    (((2, -2, "A"),), 0),
-    (((2, 2, "A"),), 0),
-    (((1, -3, "B"),), 0),
-    (((-1, -3, "B"),), 0),
-    (((1, 4, "A0"), (1, 4, "A1")), 0),
-    (((2, -1, "B0"), (2, -1, "B1")), 0),
-    (((-1, 3, "A"),), 0),
-    (((-1, -3, "A"),), 0),
-    (((2, 2, "B0"), (2, 2, "B1")), 0),
-    (((-1, 4, "A0"), (-1, 4, "A1")), 0),
-    (((2, -2, "B0"), (2, -2, "B1")), 0),
-    (((2, -3, "A"),), 0),
-    (((1, 4, "B"),), 0),
+    (((2, -2, "B0"), (2, -2, "B1")), 1),
+    (((0, 4, "A0"), (0, 4, "A1")), 9),
     (((-1, 4, "B"),), 0),
     (((2, 3, "A"),), 0),
+    (((2, -3, "A"),), 0),
+    (((2, 3, "B0"), (2, 3, "B1")), 0),
+    (((1, 4, "B"),), 0),
     (((2, 4, "A0"), (2, 4, "A1")), 0),
-    (((2, 3, "B0"), (2, 3, "B1")), 0),
     (((2, 4, "B0"), (2, 4, "B1")), 0),
+    (((-1, 4, "A0"), (-1, 4, "A1")), 0),
     (((2, -3, "B0"), (2, -3, "B1")), 0),
+    (((1, 4, "A0"), (1, 4, "A1")), 0),
 )
+
 MESSAGES = tuple(m for step, _ in STEPS for m in step)
-REACH = tuple(sorted({(d[0], h * (1 if d[1] == "+" else -1) % (NY if d[0] == "y" else NZ)) for out in ROUTES.values() for d, h, _ in out}))
+REACH = tuple(sorted({(d[0], h * (1 if d[1] == "+" else -1) % (NY if d[0] == "y" else NZ)) for out in (FIRST, *ROUTES.values()) for d, h, _ in out}))
 NUMBER = {m: i for i, m in enumerate(MESSAGES)}
 
 
@@ -360,10 +264,13 @@
     def receive(m):
         copy_of(rows_of(*m), m, greeted[0]).wait_recv()
 
-    send_on(0, 0, "A")
-    send_on(0, 0, "B")
-
-    own = win.at[0, pl.ds(mine, QD)]
+    for d, steps, m in FIRST:
+        steps = steps if d[1] == "+" else (NY if d[0] == "y" else NZ) - steps
+        copy_of(rows_of(0, 0, m[2]), m, reach(d[0], steps)).start()
+
+    def rim_part(i):
+        return win.at[0, pl.ds(mine + i * RIM, RIM)]
+
     rims = [
         pltpu.make_async_remote_copy(
             src_ref=s, dst_ref=d, send_sem=rim_send.at[i], recv_sem=rim_recv.at[i],
@@ -371,21 +278,29 @@
         )
         for i, (s, d, to) in enumerate(
             [
-                (own, own, nxt_id),
-                (own, own, prv_id),
                 (live.at[pl.ds(QD, 1)], live.at[pl.ds(0, 1)], nxt_id),
                 (live.at[pl.ds(1, 1)], live.at[pl.ds(QD + 1, 1)], prv_id),
             ]
+            + [
+                (rim_part(j), rim_part(j), to)
+                for j in range(QD // RIM)
+                for to in (nxt_id, prv_id)
+            ]
         )
     ]
-    for rim in rims:
-        rim.start()
+    def start_rims(step):
+        for j, at in enumerate(RIM_AT):
+            if at == step:
+                for rim in rims[2 + 2 * j : 4 + 2 * j] + (rims[:2] if j == 0 else []):
+                    rim.start()
+
+    start_rims(-1)
 
     def do_diag(q):
         b0, b1 = basis[2 * q], basis[2 * q + 1]
         o = jnp.zeros((64, 64), BF)
-        bdiag[q, :64] = jnp.concatenate([b0, o], axis=1)
-        bdiag[q, 64:] = jnp.concatenate([o, b1], axis=1)
+        both = [jnp.concatenate([b0, o], axis=1), jnp.concatenate([o, b1], axis=1)]
+        bdiag[q] = jnp.concatenate(both, axis=0).T
 
     def do_near(q):
         o = jnp.zeros((64, 64), BF)
@@ -456,11 +371,12 @@
             next(todo, lambda: None)()
 
     do_work(FIRST_WORK)
-    for step, pieces in STEPS:
+    for number, (step, pieces) in enumerate(STEPS):
         for m in step:
             receive(m)
         dy, dz, part = step[0]
         send_on(dy, dz, part[0] if len(step) == 2 else part)
+        start_rims(number)
         for m in step:
             rows = rows_of(*m)
             n = SPAN[m[2]][1]
@@ -479,7 +395,7 @@
         local = dot_nt(held[q], transfer[2 * q : 2 * q + 2].reshape(128, 64)) + far[q]
         coefs[q] = local.astype(BF)
     for q in range(QD):
-        total_q = dot_nt(coefs[q], bdiag[q]) + near[q]
+        total_q = dot_nn(coefs[q], bdiag[q]) + near[q]
         m0, m1 = masks(q)
         out_ref[:, 128 * q : 128 * q + 128] = jnp.where(m0 | m1, total_q, 0.0).astype(BF)
 
@@ -495,7 +411,7 @@
     n = charges.shape[0]
     result = pl.pallas_call(
         kernel,
-        out_shape=jax.ShapeDtypeStruct((R, n), BF),
+        out_shape=pltpu.VMEM((R, n), BF),
         in_specs=[pl.BlockSpec(memory_space=pltpu.HBM)] * 9,
         out_specs=pl.BlockSpec(memory_space=pltpu.VMEM),
         scratch_shapes=[
@@ -520,8 +436,8 @@
             pltpu.SemaphoreType.DMA((9,)),
             pltpu.SemaphoreType.DMA((len(MESSAGES),)),
             pltpu.SemaphoreType.DMA,
-            pltpu.SemaphoreType.DMA((4,)),
-            pltpu.SemaphoreType.DMA((4,)),
+            pltpu.SemaphoreType.DMA((2 + 2 * QD // RIM,)),
+            pltpu.SemaphoreType.DMA((2 + 2 * QD // RIM,)),
         ],
         compiler_params=pltpu.CompilerParams(
             collective_id=0, has_side_effects=True, vmem_limit_bytes=56 * 1024 * 1024

time: 35.6 us -> 33.5 us (0.941)
  the two profiles are of different devices: /device:TPU:8 before, /device:TPU:1 now
where the time goes in v3:
time: 33.5 us
  Pallas kernels  32.8 us (98%)
  local copies, waits for them, and re-layouts  0.66 us (2%)
    pallas_call x1, Pallas kernels, per_device(): pl.pallas_call(kernel, out_shape=pltpu.VMEM((R, n), BF), in_specs=[pl.Blo...  32.8 us

profile of v3, /device:TPU:1, one launch (start us, length us, event | category | flops | bytes accessed | tf_op | source)
XLA Modules:
  0.0 33.5 jit_solution(11425094902561281234)
XLA Ops:
  0.0 32.8 %shard_map.91 = bf16[32,2048]{1,0:T(8,128)(2,1)S(1)} custom-call(bf16[32,2048]{1,0:T(8,128)(2,1)} %bitcast.4, s32[32]{0:T(128)} %cnt_hbm.1, bf16[32,64,64]{2,1,0:T(8,128)(2,1)} %basis_hbm.1, bf16[32,64,64]{2,1,0:T(8,128)(2,1)} %transfer_hbm.1, bf16[32,16,64,64]{3,2,1,0:T(8,128)(2,1)} %lc_hbm.1, s32[16,32]{1,0:T(8,128)} %bitcast.5, ...), custom_call_target="tpu_custom_call" | custom-call | tf_op jit(solution)/shard_map/pallas_call | solution.py:412
  32.8 0.7 %copy.11 = bf16[2048,32]{0,1:T(8,128)(2,1)} copy(bf16[2048,32]{0,1:T(8,128)(2,1)S(1)} %bitcast.3) | data formatting | bytes 262144

commit v4 on v3

--- a/solution.py
+++ b/solution.py
@@ -67,15 +67,15 @@
     (2, 1, "A"): (("z+", 1, (2, 2, "A")),),
     (2, -1, "A"): (("z-", 1, (2, -2, "A")),),
     (1, -2, "B"): (("y+", 1, (2, -2, "B0")),),
-    (-1, -2, "B"): (("y-", 1, (2, -2, "B1")),),
     (-1, 2, "A"): (("z+", 1, (-1, 3, "A")),),
     (-1, -2, "A"): (("z-", 1, (-1, -3, "A")),),
+    (-1, -2, "B"): (("y-", 1, (2, -2, "B1")),),
     (1, 2, "A"): (("z+", 1, (1, 3, "A")),),
     (1, -2, "A"): (("z-", 1, (1, -3, "A")),),
     (0, 3, "A"): (("z+", 1, (0, 4, "A0")),),
     (0, -3, "A"): (("z-", 1, (0, 4, "A1")),),
+    (0, 4, "B"): (("y+", 2, (2, 4, "B0")), ("y-", 2, (2, 4, "B1")), ("y+", 1, (1, 4, "B")), ("y-", 1, (-1, 4, "B"))),
     (1, 3, "B"): (("y+", 1, (2, 3, "B0")),),
-    (0, 4, "B"): (("y+", 2, (2, 4, "B0")), ("y-", 2, (2, 4, "B1")), ("y+", 1, (1, 4, "B")), ("y-", 1, (-1, 4, "B"))),
     (-1, 3, "B"): (("y-", 1, (2, 3, "B1")),),
     (2, 2, "A"): (("z+", 2, (2, 4, "A0")), ("z+", 1, (2, 3, "A"))),
     (2, -2, "A"): (("z-", 2, (2, 4, "A1")), ("z-", 1, (2, -3, "A"))),
@@ -87,7 +87,7 @@
     (1, -3, "A"): (("z-", 1, (1, 4, "A1")),),
 }
 
-RIM_AT = (-1, -1, 12, 22)
+RIM_AT = (-1, -1, 8, 16)
 FIRST_WORK = 50
 STEPS = (
     (((1, 0, "B"),), 0),
@@ -119,41 +119,42 @@
     (((2, 1, "A"),), 0),
     (((2, -1, "A"),), 0),
     (((1, -2, "B"),), 0),
-    (((-1, -2, "B"),), 0),
     (((-1, 2, "A"),), 0),
     (((-1, -2, "A"),), 0),
+    (((-1, -2, "B"),), 0),
     (((1, 2, "A"),), 0),
+    (((2, 1, "B0"), (2, 1, "B1")), 0),
     (((1, -2, "A"),), 0),
-    (((2, 1, "B0"), (2, 1, "B1")), 0),
-    (((2, -1, "B0"), (2, -1, "B1")), 0),
     (((0, 3, "A"),), 0),
     (((0, -3, "A"),), 0),
+    (((2, -1, "B0"), (2, -1, "B1")), 0),
+    (((0, 4, "B0"), (0, 4, "B1")), 0),
     (((1, 3, "B"),), 0),
-    (((0, 4, "B0"), (0, 4, "B1")), 0),
-    (((-1, 3, "B"),), 0),
+    (((-1, 3, "B"),), 8),
     (((2, 2, "A"),), 0),
-    (((2, -2, "A"),), 8),
+    (((2, -2, "A"),), 0),
     (((-1, 3, "A"),), 0),
     (((-1, -3, "A"),), 0),
     (((-1, -3, "B"),), 0),
     (((1, -3, "B"),), 0),
-    (((2, 2, "B0"), (2, 2, "B1")), 1),
+    (((2, 2, "B0"), (2, 2, "B1")), 2),
     (((1, 3, "A"),), 0),
     (((1, -3, "A"),), 0),
-    (((2, -2, "B0"), (2, -2, "B1")), 1),
+    (((2, -2, "B0"), (2, -2, "B1")), 0),
     (((0, 4, "A0"), (0, 4, "A1")), 9),
     (((-1, 4, "B"),), 0),
+    (((1, 4, "B"),), 0),
     (((2, 3, "A"),), 0),
     (((2, -3, "A"),), 0),
     (((2, 3, "B0"), (2, 3, "B1")), 0),
-    (((1, 4, "B"),), 0),
+    (((-1, 4, "A0"), (-1, 4, "A1")), 0),
+    (((2, 4, "B0"), (2, 4, "B1")), 0),
     (((2, 4, "A0"), (2, 4, "A1")), 0),
-    (((2, 4, "B0"), (2, 4, "B1")), 0),
-    (((-1, 4, "A0"), (-1, 4, "A1")), 0),
     (((2, -3, "B0"), (2, -3, "B1")), 0),
     (((1, 4, "A0"), (1, 4, "A1")), 0),
 )
 
+RELAY_AT = 12
 MESSAGES = tuple(m for step, _ in STEPS for m in step)
 REACH = tuple(sorted({(d[0], h * (1 if d[1] == "+" else -1) % (NY if d[0] == "y" else NZ)) for out in (FIRST, *ROUTES.values()) for d, h, _ in out}))
 NUMBER = {m: i for i, m in enumerate(MESSAGES)}
@@ -172,7 +173,7 @@
     out_ref,
     ch, basis, transfer, lc, nb, pc, cnt, lp, pp,
     live, win, row, cpl, bdiag, near, far, held, coefs,
-    in_sem, recv_sem, send_sem, rim_recv, rim_send,
+    relay, in_sem, recv_sem, send_sem, rim_recv, rim_send, relay_recv, relay_send,
 ):
     gx = lax.axis_index("gx")
     gy = lax.axis_index("gy")
@@ -184,6 +185,9 @@
     nxt = (dev + 1) % total
     prv_id = (prv // NGY, prv % NGY)
     nxt_id = (nxt // NGY, nxt % NGY)
+    up, down = (dev + NY) % total, (dev + total - NY) % total
+    up_id = (up // NGY, up % NGY)
+    down_id = (down // NGY, down % NGY)
 
     def reach(axis, steps):
         if axis == "y":
@@ -204,7 +208,7 @@
         load.start()
 
     barrier = pltpu.get_barrier_semaphore()
-    greeted = [reach(axis, steps) for axis, steps in REACH] + [prv_id, nxt_id]
+    greeted = [reach(axis, steps) for axis, steps in REACH] + [prv_id, nxt_id, up_id, down_id]
     for d in greeted:
         pl.semaphore_signal(barrier, inc=1, device_id=d, device_id_type=MESH)
 
@@ -288,11 +292,46 @@
             ]
         )
     ]
+    def detour(j, forward):
+        k = 2 + 2 * j + (0 if forward else 1)
+        some = dev != (total - 1 if forward else 0)
+        far = y == (NY - 1 if forward else 0)
+        held_there = (y == (0 if forward else NY - 1)) & (dev != (total - NY if forward else NY - 1))
+        slot = ((NY - 1) if forward else 0) * QD + j * RIM
+        part = relay.at[pl.ds(j * RIM, RIM)]
+        there = pltpu.make_async_remote_copy(
+            src_ref=rim_part(j), dst_ref=part, send_sem=rim_send.at[k],
+            recv_sem=relay_recv.at[j], device_id=reach("y", 1 if forward else NY - 1),
+            device_id_type=MESH,
+        )
+        onward = pltpu.make_async_remote_copy(
+            src_ref=part, dst_ref=win.at[0, pl.ds(slot, RIM)], send_sem=relay_send.at[j],
+            recv_sem=rim_recv.at[k], device_id=up_id if forward else down_id,
+            device_id_type=MESH,
+        )
+        return rims[k], some & jnp.logical_not(far), some & far, there, held_there, onward
+
+    detours = [detour(j, forward) for j in range(2) for forward in (True, False)]
+
     def start_rims(step):
         for j, at in enumerate(RIM_AT):
-            if at == step:
-                for rim in rims[2 + 2 * j : 4 + 2 * j] + (rims[:2] if j == 0 else []):
-                    rim.start()
+            if at == step and j >= 2:
+                for k in (2 + 2 * j, 3 + 2 * j):
+                    pl.when(dev != (total - 1 if k % 2 == 0 else 0))(rims[k].start)
+            elif at == step:
+                for straight, near_by, far, there, _, _ in detours[2 * j : 2 * j + 2]:
+                    pl.when(far)(there.start)
+                    pl.when(near_by)(straight.start)
+        if step == -1:
+            for k in range(2):
+                pl.when(dev != (total - 1 if k % 2 == 0 else 0))(rims[k].start)
+        if step == RELAY_AT:
+            for _, _, _, there, held_there, onward in detours:
+
+                @pl.when(held_there)
+                def _(there=there, onward=onward):
+                    there.wait_recv()
+                    onward.start()
 
     start_rims(-1)
 
@@ -345,8 +384,8 @@
         far[q] = jnp.concatenate([leaf_sum(2 * q), leaf_sum(2 * q + 1)], axis=1)
 
     def take_rims():
-        for rim in rims:
-            rim.wait_recv()
+        for k, rim in enumerate(rims):
+            pl.when(dev != (0 if k % 2 == 0 else total - 1))(rim.wait_recv)
         live[0] = jnp.where(dev > 0, live[0], zero)
         live[QD + 1] = jnp.where(dev < total - 1, live[QD + 1], zero)
 
@@ -399,8 +438,10 @@
         m0, m1 = masks(q)
         out_ref[:, 128 * q : 128 * q + 128] = jnp.where(m0 | m1, total_q, 0.0).astype(BF)
 
-    for rim in rims:
-        rim.wait_send()
+    for k, rim in enumerate(rims):
+        pl.when(dev != (total - 1 if k % 2 == 0 else 0))(rim.wait_send)
+    for _, _, _, _, held_there, onward in detours:
+        pl.when(held_there)(onward.wait_send)
     copy_of(pl.ds(0, ROW_UNITS - UD), MESSAGES[0], greeted[0]).wait_send()
 
 
@@ -433,11 +474,14 @@
             pltpu.VMEM((QD, R, 128), F32),
             pltpu.VMEM((QD, R, 64), BF),
             pltpu.VMEM((QD, R, 128), BF),
+            pltpu.VMEM((2 * RIM, R, 128), BF),
             pltpu.SemaphoreType.DMA((9,)),
             pltpu.SemaphoreType.DMA((len(MESSAGES),)),
             pltpu.SemaphoreType.DMA,
             pltpu.SemaphoreType.DMA((2 + 2 * QD // RIM,)),
             pltpu.SemaphoreType.DMA((2 + 2 * QD // RIM,)),
+            pltpu.SemaphoreType.DMA((2,)),
+            pltpu.SemaphoreType.DMA((2,)),
         ],
         compiler_params=pltpu.CompilerParams(
             collective_id=0, has_side_effects=True, vmem_limit_bytes=56 * 1024 * 1024

time: 33.5 us -> 32.4 us (0.967)
  the two profiles are of different devices: /device:TPU:1 before, /device:TPU:8 now
where the time goes in v4:
time: 32.4 us; the launch traced here: 32.2 us
  Pallas kernels  31.5 us (97%)
  local copies, waits for them, and re-layouts  0.66 us (2%)
    pallas_call x1, Pallas kernels, per_device(): pl.pallas_call(kernel, out_shape=pltpu.VMEM((R, n), BF), in_specs=[pl.Blo...  31.5 us
    unnamed x1, local copies, waits for them, and re-layouts  0.66 us

profile of v4, /device:TPU:8, one launch (start us, length us, event | category | flops | bytes accessed | tf_op | source)
XLA Modules:
  0.0 32.2 jit_solution(15800647700029226644)
XLA Ops:
  0.0 31.5 %shard_map.91 = bf16[32,2048]{1,0:T(8,128)(2,1)S(1)} custom-call(bf16[32,2048]{1,0:T(8,128)(2,1)} %bitcast.4, s32[32]{0:T(128)} %cnt_hbm.1, bf16[32,64,64]{2,1,0:T(8,128)(2,1)} %basis_hbm.1, bf16[32,64,64]{2,1,0:T(8,128)(2,1)} %transfer_hbm.1, bf16[32,16,64,64]{3,2,1,0:T(8,128)(2,1)} %lc_hbm.1, s32[16,32]{1,0:T(8,128)} %bitcast.5, ...), custom_call_target="tpu_custom_call" | custom-call | tf_op jit(solution)/shard_map/pallas_call | solution.py:453
  31.5 0.7 %copy.11 = bf16[2048,32]{0,1:T(8,128)(2,1)} copy(bf16[2048,32]{0,1:T(8,128)(2,1)S(1)} %bitcast.3) | data formatting | bytes 262144

commit v5 on v4

--- a/solution.py
+++ b/solution.py
@@ -172,7 +172,7 @@
     ch_hbm, cnt_hbm, basis_hbm, transfer_hbm, lc_hbm, lp_hbm, nb_hbm, pc_hbm, pp_hbm,
     out_ref,
     ch, basis, transfer, lc, nb, pc, cnt, lp, pp,
-    live, win, row, cpl, bdiag, near, far, held, coefs,
+    live, win, row, cpl, bdiag, near, far, held, coefs, down_t,
     relay, in_sem, recv_sem, send_sem, rim_recv, rim_send, relay_recv, relay_send,
 ):
     gx = lax.axis_index("gx")
@@ -340,6 +340,7 @@
         o = jnp.zeros((64, 64), BF)
         both = [jnp.concatenate([b0, o], axis=1), jnp.concatenate([o, b1], axis=1)]
         bdiag[q] = jnp.concatenate(both, axis=0).T
+        down_t[q] = transfer[2 * q : 2 * q + 2].reshape(128, 64).T
 
     def do_near(q):
         o = jnp.zeros((64, 64), BF)
@@ -421,27 +422,28 @@
             n = SPAN[m[2]][1]
             row[1, rows] = swap(row[0, rows].reshape(n * 16, 128)).reshape(n, 16, 128)
         do_work(pieces)
+        if number == len(STEPS) - 5:
+            loads[6].wait()
+            for k, rim in enumerate(rims):
+                pl.when(dev != (total - 1 if k % 2 == 0 else 0))(rim.wait_send)
+            for _, _, _, _, held_there, onward in detours:
+                pl.when(held_there)(onward.wait_send)
     for unit in todo:
         unit()
 
-    loads[6].wait()
     for q in range(QD):
         lhs = jnp.concatenate(
             [pick_parents(pp[q, 2 * i], pp[q, 2 * i + 1]) for i in range(8)], axis=1
         )
         held[q] = dot_nt(lhs, cpl[q]).astype(BF)
     for q in range(QD):
-        local = dot_nt(held[q], transfer[2 * q : 2 * q + 2].reshape(128, 64)) + far[q]
+        local = dot_nn(held[q], down_t[q]) + far[q]
         coefs[q] = local.astype(BF)
     for q in range(QD):
         total_q = dot_nn(coefs[q], bdiag[q]) + near[q]
         m0, m1 = masks(q)
         out_ref[:, 128 * q : 128 * q + 128] = jnp.where(m0 | m1, total_q, 0.0).astype(BF)
 
-    for k, rim in enumerate(rims):
-        pl.when(dev != (total - 1 if k % 2 == 0 else 0))(rim.wait_send)
-    for _, _, _, _, held_there, onward in detours:
-        pl.when(held_there)(onward.wait_send)
     copy_of(pl.ds(0, ROW_UNITS - UD), MESSAGES[0], greeted[0]).wait_send()
 
 
@@ -474,6 +476,7 @@
             pltpu.VMEM((QD, R, 128), F32),
             pltpu.VMEM((QD, R, 64), BF),
             pltpu.VMEM((QD, R, 128), BF),
+            pltpu.VMEM((QD, 64, 128), BF),
             pltpu.VMEM((2 * RIM, R, 128), BF),
             pltpu.SemaphoreType.DMA((9,)),
             pltpu.SemaphoreType.DMA((len(MESSAGES),)),

time: 32.4 us -> 32.3 us (level)
  no operation moved by 1% of the time
where the time goes in v5:
time: 32.3 us; the launch traced here: 32 us
  Pallas kernels  31.4 us (97%)
  local copies, waits for them, and re-layouts  0.66 us (2%)
    pallas_call x1, Pallas kernels, per_device(): pl.pallas_call(kernel, out_shape=pltpu.VMEM((R, n), BF), in_specs=[pl.Blo...  31.4 us
    unnamed x1, local copies, waits for them, and re-layouts  0.66 us

profile of v5, /device:TPU:8, one launch (start us, length us, event | category | flops | bytes accessed | tf_op | source)
XLA Modules:
  0.0 32.0 jit_solution(145128699786430796)
XLA Ops:
  0.0 31.4 %shard_map.91 = bf16[32,2048]{1,0:T(8,128)(2,1)S(1)} custom-call(bf16[32,2048]{1,0:T(8,128)(2,1)} %bitcast.4, s32[32]{0:T(128)} %cnt_hbm.1, bf16[32,64,64]{2,1,0:T(8,128)(2,1)} %basis_hbm.1, bf16[32,64,64]{2,1,0:T(8,128)(2,1)} %transfer_hbm.1, bf16[32,16,64,64]{3,2,1,0:T(8,128)(2,1)} %lc_hbm.1, s32[16,32]{1,0:T(8,128)} %bitcast.5, ...), custom_call_target="tpu_custom_call" | custom-call | tf_op jit(solution)/shard_map/pallas_call | solution.py:455
  31.4 0.7 %copy.11 = bf16[2048,32]{0,1:T(8,128)(2,1)} copy(bf16[2048,32]{0,1:T(8,128)(2,1)S(1)} %bitcast.3) | data formatting | bytes 262144
